TPU v7x, 32 devices: a whole 2x2x4 slice. The times are simulated.
32 devices in a mesh: dom: 8 (over y, x, core), orient: 4 (over z).
Axes of the slice: x: 2, y: 2, z: 4, core: 2. Of those that a mesh axis runs over, the one named last changes fastest.
Arguments:
- particles: bfloat16 [64, 2, 8192], P('dom'), may hold values from -4 to 4
- references: bfloat16 [64, 2, 8192], P('orient'), may hold values from -1.7 to 1.7
- phases: float32 [16, 8192], replicated, may hold values from -3.1416 to 3.1416
- mask: int32 [64, 64], P('dom', 'orient'), may hold values from 0 to 1, as said below
- ctf_group: int32 [64], replicated, may hold values from 0 to 63
- ctf_table: float32 [64, 64], replicated, may hold values from 0.1 to 1
- shell_index: int32 [8192], replicated, may hold values from 0 to 63
- sigma2: float32 [64], replicated, may hold values from 8 to 32
Outputs:
- posterior: float32 [64, 16, 64], P('dom', None, 'orient')
- image_sums: float32 [64, 2, 8192], P('orient', None, 'dom')
- ctf_weights: float32 [64, 64], P('orient')
- shell_noise: float32 [64], replicated
Inputs may be any that keep to these rules, and one draw needn't show every extreme that they name: `mask`: every particle allows at least one orientation.
All inputs are finite; a program needn't handle non-finite values.
Results may differ from a plain program's by a relative error of at most 0.0041.
Values may be sent and summed in bfloat16 or wider, within the bound.
No kernel may reach another device: no remote copies, remote signals or barrier semaphores. Data moves between devices by JAX's collectives and lax.ppermute only.
A program may use at most 192 MiB of HBM per device.

v0:
```python
import jax
import jax.numpy as jnp
from jax import lax
from jax.sharding import PartitionSpec as P

trans_block = 2


def make_images(planes, ctf_pix, cosine, sine_part):
    real_part = planes[:, 0][:, None, :]
    imag_part = planes[:, 1][:, None, :]
    shifted_real = real_part * cosine[None] - imag_part * sine_part[None]
    shifted_imag = real_part * sine_part[None] + imag_part * cosine[None]
    factor = ctf_pix[:, None, :]
    return jnp.stack([factor * shifted_real, factor * shifted_imag], axis=2).astype(jnp.bfloat16)


def on_device(particles, references, phases, mask, ctf_group, ctf_table, shell_index, sigma2):
    highest = lax.Precision.HIGHEST
    part_dev = particles.shape[0]
    ori_dev = references.shape[0]
    pixels = shell_index.shape[0]
    shells = ctf_table.shape[1]
    trans_count = phases.shape[0]
    blocks = trans_count // trans_block
    dom_size = lax.axis_size("dom")
    width = pixels // dom_size
    dom_index = lax.axis_index("dom")
    columns = lax.all_to_all(particles, "dom", split_axis=2, concat_axis=0, tiled=True)
    shell_pick = (shell_index[:, None] == jnp.arange(shells, dtype=jnp.int32)[None, :]).astype(
        jnp.float32
    )
    group_pick = (
        ctf_group[:, None] == jnp.arange(ctf_table.shape[0], dtype=jnp.int32)[None, :]
    ).astype(jnp.float32)
    ctf_all = jnp.dot(group_pick, ctf_table, precision=highest)
    ctf_rows = lax.dynamic_slice_in_dim(ctf_all, dom_index * part_dev, part_dev, 0)
    ctf_pix = jnp.dot(ctf_rows, shell_pick.T, precision=highest)
    sigma_pix = jnp.dot(shell_pick, sigma2, precision=highest)
    refs_wide = references.astype(jnp.float32)
    weighted = (refs_wide / sigma_pix).astype(jnp.bfloat16)
    ref_norm = jnp.dot(jnp.sum(refs_wide * refs_wide, axis=1), shell_pick, precision=highest)
    energy = ref_norm / sigma2
    ctf_square = ctf_rows * ctf_rows
    quadratic = 0.5 * jnp.dot(ctf_square, energy.T, precision=highest)
    planes = particles.astype(jnp.float32)
    cosines = jnp.cos(phases)
    sine_rows = jnp.sin(phases)

    def score_block(index):
        first = index * trans_block
        images = make_images(
            planes,
            ctf_pix,
            lax.dynamic_slice_in_dim(cosines, first, trans_block, 0),
            lax.dynamic_slice_in_dim(sine_rows, first, trans_block, 0),
        )
        cross = jnp.einsum("ptcx,ocx->pto", images, weighted, preferred_element_type=jnp.float32)
        return cross - quadratic[:, None, :]

    stacked = lax.map(score_block, jnp.arange(blocks, dtype=jnp.int32))
    scores = jnp.moveaxis(stacked, 0, 1).reshape(part_dev, trans_count, ori_dev)
    scores = jnp.where((mask == 1)[:, None, :], scores, -1e30)
    local_peak = jnp.max(scores, axis=(1, 2))
    peak = lax.pmax(local_peak, "orient")
    total = lax.psum(jnp.sum(jnp.exp(scores - peak[:, None, None]), axis=(1, 2)), "orient")
    posterior = jnp.exp(scores - peak[:, None, None]) / total[:, None, None]
    post_half = posterior.astype(jnp.bfloat16)
    weight_rows = jnp.sum(posterior, axis=1)
    ctf_part = jnp.dot(weight_rows.T, ctf_square, precision=highest)
    part_norm = jnp.dot(jnp.sum(planes * planes, axis=1), shell_pick, precision=highest)
    term_one = jnp.sum(part_norm * jnp.sum(weight_rows, axis=1)[:, None], axis=0)
    term_three = jnp.sum(ctf_part * ref_norm, axis=0)
    start_pix = dom_index * width
    pick_cols = lax.dynamic_slice_in_dim(shell_pick, start_pix, width, 0)
    cos_cols = lax.dynamic_slice_in_dim(cosines, start_pix, width, 1)
    sine_cols = lax.dynamic_slice_in_dim(sine_rows, start_pix, width, 1)
    ctf_cols = jnp.dot(ctf_all, pick_cols.T, precision=highest)
    piece = lax.all_gather(post_half, "dom", axis=0, tiled=True)
    rows_wide = columns.astype(jnp.float32)

    def add_columns(index, running):
        first = index * trans_block
        images = make_images(
            rows_wide,
            ctf_cols,
            lax.dynamic_slice_in_dim(cos_cols, first, trans_block, 0),
            lax.dynamic_slice_in_dim(sine_cols, first, trans_block, 0),
        )
        weights = lax.dynamic_slice_in_dim(piece, first, trans_block, 1)
        return running + jnp.einsum(
            "pto,ptcx->ocx", weights, images, preferred_element_type=jnp.float32
        )

    image_sums = lax.fori_loop(0, blocks, add_columns, jnp.zeros((ori_dev, 2, width), jnp.float32))
    ref_cols = lax.dynamic_slice_in_dim(refs_wide, start_pix, width, 2)
    term_two = -2.0 * jnp.dot(
        jnp.sum(image_sums * ref_cols, axis=(0, 1)), pick_cols, precision=highest
    )
    ctf_weights = lax.psum(ctf_part, "dom")
    shell_total = lax.psum(term_one + term_two + term_three, ("dom", "orient"))
    divisor = part_dev * dom_size * pixels / shells
    return (posterior, image_sums, ctf_weights, shell_total / divisor)


def solution(mesh):
    return jax.shard_map(
        on_device,
        mesh=mesh,
        in_specs=(
            P("dom", None, None),
            P("orient", None, None),
            P(),
            P("dom", "orient"),
            P(),
            P(),
            P(),
            P(),
        ),
        out_specs=(P("dom", None, "orient"), P("orient", None, "dom"), P("orient", None), P()),
        check_vma=False,
    )
```

profile of v0, /device:TPU:0, one launch (start us, length us, event | category | flops | bytes accessed | tf_op | source)
XLA Modules:
  0.0 171.8 jit_solution(13517294230878619158)
XLA Ops:
  0.6 8.7 %copy.35 = bf16[8,2,8192]{0,1,2:T(2,128)(2,1)} copy(bf16[8,2,8192]{2,1,0:T(2,128)(2,1)} %param.12) | data formatting | bytes 524288 | tf_op args[0]
  9.4 6.4 %reshape.91 = bf16[8,2,8192]{2,1,0:T(2,128)(2,1)} reshape(bf16[8192,2,8]{2,1,0:T(2,128)(2,1)} %bitcast.82) | data formatting | bytes 524288
  15.8 5.3 %all-to-all-start = ((bf16[8,2,8192]{2,1,0:T(2,128)(2,1)}), bf16[8,2,8192]{2,1,0:T(2,128)(2,1)S(1)}, u32[]{:S(2)}, u32[]{:S(2)}) async-start(bf16[8,2,8192]{2,1,0:T(2,128)(2,1)} %reshape.91), calls=%async_computation | async-start | bytes 524288 | tf_op jit(solution)/shard_map/all_to_all | solution.py:29
  21.5 1.1 iota_compare_fusion
  22.6 0.7 fusion.18
  23.3 0.3 copy_convert_fusion
  23.6 1.2 multiply_reduce_fusion
  24.8 1.1 fusion.17
  25.9 0.2 fusion.34
  26.1 1.5 fusion.19
  27.7 0.7 convolution_multiply_fusion
  28.4 2.8 %fusion.52 = (f32[16,8192]{1,0:T(8,128)S(1)}, f32[16,8192]{1,0:T(8,128)S(1)}) fusion(f32[16,8192]{1,0:T(8,128)} %param.14), kind=kLoop, calls=%fused_computation.85 | loop fusion | bytes 1572864 | tf_op jit(solution)/shard_map/sin | solution.py:48
  31.2 21.1 %while.24 = (s32[]{:T(128)}, f32[8,8,2,16]{3,1,2,0:T(8,128)S(1)}, f32[8,8192]{1,0:T(8,128)S(1)}, f32[8,2,8192]{2,0,1:T(8,128)S(1)}, s32[8]{0:T(128)S(1)}, /*inde...) while((s32[]{:T(128)}, f32[8,8,2,16]{3,1,2,0:T(8,128)S(1)}, ...), condition=%wide.region_2.3_spmd, body=%wide.region_1.2_spmd.sunk | while | flops 9961734 | bytes 5912823 | solution.py:61
  31.2 0.6 dynamic_slice.86
  32.8 0.7 copy-done.3
  33.5 0.3 fusion.67
  33.8 0.6 dynamic_slice.86
  35.4 0.7 copy-done.3
  36.1 0.3 fusion.67
  36.5 0.6 dynamic_slice.86
  38.0 0.7 copy-done.3
  38.8 0.3 fusion.67
  39.1 0.6 dynamic_slice.86
  40.7 0.7 copy-done.3
  41.4 0.3 fusion.67
  41.7 0.6 dynamic_slice.86
  43.3 0.7 copy-done.3
  44.0 0.3 fusion.67
  44.4 0.6 dynamic_slice.86
  45.9 0.7 copy-done.3
  46.7 0.3 fusion.67
  47.0 0.6 dynamic_slice.86
  48.6 0.7 copy-done.3
  49.3 0.3 fusion.67
  49.7 0.6 dynamic_slice.86
  51.2 0.7 copy-done.3
  52.0 0.3 fusion.67
  52.5 12.0 %pmax.7 = f32[8]{0:T(128)S(1)} all-reduce(f32[8]{0:T(128)S(1)} %select_reduce_fusion), channel_id=1, replica_groups=mesh['dom'=8,'orient'=4] {'orient'}, use_global_device_ids=true, to_apply=%region_4.5 | all-reduce | flops 8 | bytes 64 | tf_op jit(solution)/shard_map/pmax | solution.py:65
  64.4 0.2 fusion.33
  64.7 8.4 %psum.21 = f32[8]{0:T(128)S(1)} all-reduce(f32[8]{0:T(128)S(1)} %fusion.33), channel_id=1, replica_groups=mesh['dom'=8,'orient'=4] {'orient'}, use_global_device_ids=true, to_apply=%region_6.7 | all-reduce | flops 8 | bytes 64 | tf_op jit(solution)/shard_map/psum | solution.py:66
  73.1 0.2 fusion.50
  73.3 0.7 fusion.51
  74.0 9.8 %all_gather.3 = bf16[64,16,16]{2,1,0:T(8,128)(2,1)S(1)} all-gather(bf16[8,16,16]{2,1,0:T(8,128)(2,1)S(1)} %get-tuple-element.279), channel_id=1, replica_groups=mesh['dom'=8,'orient'=4] {'dom'}, dimensions={0}, use_global_device_ids=true | all-gather | bytes 36864 | tf_op jit(solution)/shard_map/all_gather | solution.py:79
  83.8 0.3 copy.37
  84.1 0.2 multiply_reduce_fusion.3
  84.3 14.2 %psum.22 = f32[16,64]{1,0:T(8,128)} all-reduce(f32[16,64]{1,0:T(8,128)S(1)} %get-tuple-element.298), channel_id=1, replica_groups=mesh['dom'=8,'orient'=4] {'dom'}, use_global_device_ids=true, to_apply=%region_10.11 | all-reduce | flops 1024 | bytes 8192 | tf_op jit(solution)/shard_map/psum | solution.py:100
  98.5 1.8 %fusion.21 = f32[64]{0:T(128)S(1)} fusion(f32[8,8192]{1,0:T(8,128)S(1)} %multiply_reduce_fusion.1, s32[8192]{0:T(1024)} %param.18, f32[8]{0:T(128)S(1)} %get-tuple-element.245), kind=kOutput, calls=%fused_computation.38 | convolution fusion | flops 50856896 | bytes 295200 | tf_op jit(solution)/shard_map/dot_general | solution.py:71
  100.3 1.1 fusion.30
  101.5 5.9 %reshape.92 = bf16[8192,2,8]{2,1,0:T(2,128)(2,1)} reshape(bf16[8,2,8192]{2,1,0:T(2,128)(2,1)S(1)} %all-to-all-done) | data formatting | bytes 524288
  107.4 8.3 %convert_bitcast_fusion = f32[8,8,2,1024]{1,2,3,0:T(2,128)} fusion(bf16[8,2,8,1024]{0,1,3,2:T(2,128)(2,1)} %bitcast.81), kind=kLoop, calls=%fused_computation.30 | loop fusion | flops 131072 | bytes 786432 | tf_op jit(solution)/shard_map/convert_element_type | solution.py:80
  115.7 10.1 %copy.36 = f32[8,8,2,1024]{3,1,0,2:T(8,128)S(1)} copy(f32[8,8,2,1024]{1,2,3,0:T(2,128)} %convert_bitcast_fusion) | data formatting | bytes 1048576 | tf_op jit(solution)/shard_map/convert_element_type | solution.py:80
  125.8 4.0 %while.25 = (s32[]{:T(128)}, f32[16,2,1024]{2,0,1:T(8,128)S(1)}, bf16[64,16,16]{0,2,1:T(8,128)(2,1)S(1)}, f32[64,1024]{1,0:T(8,128)S(1)}, f32[64,2,1024]{2,0,1:T...) while((s32[]{:T(128)}, f32[16,2,1024]{2,0,1:T(8,128)S(1)}, ...), condition=%wide.region_8.9_spmd.clone, body=%wide.region_7.8_spmd.clone.sunk | while | flops 10813447 | bytes 3203245 | solution.py:95
  126.1 0.2 fusion.70
  126.6 0.2 fusion.70
  127.1 0.2 fusion.70
  127.6 0.2 fusion.70
  128.1 0.2 fusion.70
  128.6 0.2 fusion.70
  129.1 0.2 fusion.70
  129.6 0.2 fusion.70
  129.8 0.8 copy.38
  130.6 1.0 fusion.24
  131.6 39.7 %psum.23 = f32[64]{0:T(128)S(1)} all-reduce(f32[64]{0:T(128)S(1)} %fusion.24), channel_id=1, replica_groups=mesh['dom'=8,'orient'=4] {'dom','orient'}, use_global_device_ids=true, to_apply=%region_16.17 | all-reduce | flops 64 | bytes 512 | tf_op jit(solution)/shard_map/psum | solution.py:101
  171.3 0.5 broadcast_multiply_fusion
  (97 shorter events, 4.4 us)
Async XLA Ops:
  0.6 25.3 %copy-start = (f32[64,64]{1,0:T(8,128)S(1)}, f32[64,64]{1,0:T(8,128)}, u32[]{:S(2)}) copy-start(f32[64,64]{1,0:T(8,128)} %param.17) | copy-start | bytes 49156
  9.4 11.8 %copy-start.1 = (bf16[8,2,8192]{2,1,0:T(2,128)(2,1)S(1)}, bf16[8,2,8192]{2,1,0:T(2,128)(2,1)}, u32[]{:S(2)}) copy-start(bf16[8,2,8192]{2,1,0:T(2,128)(2,1)} %param.12) | copy-start | bytes 786436
  9.4 12.1 %copy-start.4 = (s32[8192]{0:T(1024)S(1)}, s32[8192]{0:T(1024)}, u32[]{:S(2)}) copy-start(s32[8192]{0:T(1024)} %param.18) | copy-start | bytes 98308
  15.8 6.8 %copy-start.7 = (f32[64]{0:T(128)S(1)}, f32[64]{0:T(128)}, u32[]{:S(2)}) copy-start(f32[64]{0:T(128)} %param.19) | copy-start | bytes 772
  15.8 7.5 %copy-start.2 = (bf16[16,2,8192]{2,1,0:T(2,128)(2,1)S(1)}, bf16[16,2,8192]{2,1,0:T(2,128)(2,1)}, u32[]{:S(2)}) copy-start(bf16[16,2,8192]{2,1,0:T(2,128)(2,1)} %param.13) | copy-start | bytes 1572868
  15.8 85.6 %all-to-all-start = ((bf16[8,2,8192]{2,1,0:T(2,128)(2,1)}), bf16[8,2,8192]{2,1,0:T(2,128)(2,1)S(1)}, u32[]{:S(2)}, u32[]{:S(2)}) async-start(bf16[8,2,8192]{2,1,0:T(2,128)(2,1)} %reshape.91), calls=%async_computation | async-start | bytes 524288 | tf_op jit(solution)/shard_map/all_to_all | solution.py:29
  22.6 3.4 %copy-start.6 = (s32[64]{0:T(128)S(1)}, s32[64]{0:T(128)}, u32[]{:S(2)}) copy-start(s32[64]{0:T(128)} %param.16) | copy-start | bytes 772
  31.2 21.1 %copy-start.5 = (s32[8,16]{1,0:T(8,128)S(1)}, s32[8,16]{1,0:T(8,128)}, u32[]{:S(2)}) copy-start(s32[8,16]{1,0:T(8,128)} %param.15) | copy-start | bytes 1540
  32.5 1.0 copy-start.3
  32.5 1.0 copy-start.8
  35.1 1.0 copy-start.3
  35.1 1.0 copy-start.8
  37.7 1.0 copy-start.3
  37.7 1.0 copy-start.8
  40.4 1.0 copy-start.3
  40.4 1.0 copy-start.8
  43.0 1.0 copy-start.3
  43.0 1.0 copy-start.8
  45.6 1.0 copy-start.3
  45.7 1.0 copy-start.8
  48.3 1.0 copy-start.3
  48.3 1.0 copy-start.8
  50.9 1.0 copy-start.3
  50.9 1.0 copy-start.8
where the time goes:
time: 174 us; the launch traced here: 172 us
  blocking collectives  84.1 us (48%)
  local copies, waits for them, and re-layouts  47.1 us (27%)
  other arithmetic  15.6 us (9%)
  matrix products  13.1 us (8%)
  loops' own time  5.91 us (3%)
  starting transfers between devices  5.3 us (3%)
    psum x1, blocking collectives, on_device(): shell_total = lax.psum(term_one + term_two + term_three, ('dom', 'orient'))  39.7 us
    unnamed x19, local copies, waits for them, and re-layouts  22.2 us
    psum x1, blocking collectives, on_device(): ctf_weights = lax.psum(ctf_part, 'dom')  14.2 us
    pmax x1, blocking collectives, on_device(): peak = lax.pmax(local_peak, 'orient')  12 us
    convert_element_type x1, local copies, waits for them, and re-layouts, on_device(): rows_wide = columns.astype(jnp.float32)  10.1 us
    all_gather x1, blocking collectives, on_device(): piece = lax.all_gather(post_half, 'dom', axis=0, tiled=True)  9.8 us
    psum x1, blocking collectives, on_device(): lax.psum(jnp.sum(jnp.exp(scores - peak[:, None, None]), axis=(1, 2)), 'or...  8.37 us
    convert_element_type x1, other arithmetic, on_device(): rows_wide = columns.astype(jnp.float32)  8.29 us
  transfers between devices with their start and end apart: 1, of which 0 were waited for; matrix products, arithmetic and copies ran while one was open for 14% of the time, Pallas kernels for 0%

commit v1 on v0

v1 whole, which is shorter than its diff:
```python
import functools

import jax
import jax.numpy as jnp
from jax import lax
from jax.experimental import pallas as pl
from jax.experimental.pallas import tpu as pltpu
from jax.sharding import PartitionSpec as P

f32 = jnp.float32
bf16 = jnp.bfloat16
highest = lax.Precision.HIGHEST
vmem_bytes = 48 * 1024 * 1024
lanes = 128
stat_rows = 8

sin_terms = (0.9999999765, -0.1666664763, 0.008332899647, -0.0001980088726, 2.590467298e-06)
cos_terms = (0.9999999998, -0.4999999942, 0.04166663615, -0.001388836116, 2.476015062e-05, -2.605130164e-07)


def horner(terms, z):
    total = jnp.full_like(z, terms[-1])
    for term in terms[-2::-1]:
        total = total * z + term
    return total


def sin_cos(angle):
    half = angle * 0.5
    z = half * half
    s = half * horner(sin_terms, z)
    c = horner(cos_terms, z)
    twice = s + s
    return twice * c, 1.0 - twice * s


def pieces(x, count):
    out = []
    rest = x
    for step in range(count):
        piece = rest.astype(bf16)
        out.append(piece)
        if step + 1 < count:
            rest = rest - piece.astype(f32)
    return out


def nt(a, b, **kw):
    return lax.dot_general(a, b, (((1,), (1,)), ((), ())), preferred_element_type=f32, **kw)


def tn(a, b, **kw):
    return lax.dot_general(a, b, (((0,), (0,)), ((), ())), preferred_element_type=f32, **kw)


def nn(a, b, **kw):
    return lax.dot_general(a, b, (((1,), (0,)), ((), ())), preferred_element_type=f32, **kw)


def one_hot(index_row, shells):
    rows = lax.broadcasted_iota(jnp.int32, (shells, index_row.shape[1]), 0)
    return jnp.where(rows == index_row, 1.0, 0.0).astype(bf16)


def write_images(img_ref, row0, col0, scaled_r, scaled_m, cosine, sine):
    trans, width = cosine.shape
    for i in range(scaled_r.shape[0]):
        r = jnp.broadcast_to(scaled_r[i : i + 1], (trans, width))
        m = jnp.broadcast_to(scaled_m[i : i + 1], (trans, width))
        rows = pl.ds(row0 + i * trans, trans)
        img_ref[0, rows, pl.ds(col0, width)] = (r * cosine - m * sine).astype(bf16)
        img_ref[1, rows, pl.ds(col0, width)] = (r * sine + m * cosine).astype(bf16)


def score_kernel(
    chunk,
    group_ref,
    part_ref,
    refs_ref,
    phase_ref,
    shell_ref,
    mask_ref,
    table_ref,
    sigma_ref,
    send_ref,
    stat_ref,
    e_ref,
    img_ref,
    planes_ref,
    hot_ref,
    rows_ref,
    norm_ref,
    score_ref,
):
    part_dev, _, pixels = part_ref.shape
    ori_dev = refs_ref.shape[0]
    trans = phase_ref.shape[0]
    shells = table_ref.shape[1]
    dests, _, _, width = send_ref.shape
    pairs = part_dev * trans
    blocks = pixels // chunk
    first = lax.axis_index("dom") * part_dev

    for i in range(part_dev):
        rows_ref[pl.ds(i, 1), :] = table_ref[pl.ds(group_ref[first + i], 1), :]
    ctf_rows = rows_ref[...]
    sigma = sigma_ref[...]
    inverse = jnp.broadcast_to(1.0 / sigma, (8, shells))
    table = jnp.concatenate(
        [p.astype(f32) for p in pieces(ctf_rows, 3)] + [p.astype(f32) for p in pieces(inverse, 3)], axis=0
    ).astype(bf16)
    score_ref[...] = jnp.zeros_like(score_ref)
    norm_ref[...] = jnp.zeros_like(norm_ref)

    def first_pass(step, carry):
        col0 = pl.multiple_of(step * chunk, chunk)
        cols = pl.ds(col0, chunk)
        hot = one_hot(shell_ref[:, cols], shells)
        hot_ref[:, cols] = hot
        picked = nn(table, hot)
        n = part_dev
        ctf_pix = picked[0:n] + picked[n : 2 * n] + picked[2 * n : 3 * n]
        inv_sigma = picked[3 * n : 3 * n + 1] + picked[3 * n + 8 : 3 * n + 9] + picked[3 * n + 16 : 3 * n + 17]
        part = part_ref[:, :, cols].astype(f32)
        part_r = part[:, 0, :]
        part_m = part[:, 1, :]
        refs = refs_ref[:, :, cols].astype(f32)
        refs_r = refs[:, 0, :]
        refs_m = refs[:, 1, :]
        planes_ref[0, :, cols] = refs_r.astype(bf16)
        planes_ref[1, :, cols] = refs_m.astype(bf16)
        squares = pieces(refs_r * refs_r + refs_m * refs_m, 2) + pieces(part_r * part_r + part_m * part_m, 2)
        for k, offset in enumerate((0, ori_dev, 2 * ori_dev, 2 * ori_dev + part_dev)):
            size = squares[k].shape[0]
            norm_ref[pl.ds(offset, size), :] += nt(squares[k], hot)
        sine, cosine = sin_cos(phase_ref[:, cols])
        write_images(img_ref, 0, col0, part_r * ctf_pix, part_m * ctf_pix, cosine, sine)
        score_ref[...] += nt((refs_r * inv_sigma).astype(bf16), img_ref[0, :, cols]) + nt(
            (refs_m * inv_sigma).astype(bf16), img_ref[1, :, cols]
        )
        return carry

    lax.fori_loop(0, blocks, first_pass, 0)

    ref_norm = norm_ref[0:ori_dev, :] + norm_ref[ori_dev : 2 * ori_dev, :]
    part_norm = norm_ref[2 * ori_dev : 2 * ori_dev + part_dev, :] + norm_ref[2 * ori_dev + part_dev :, :]
    ctf_square = ctf_rows * ctf_rows
    square_wide = jnp.broadcast_to(ctf_square[:, None, :], (part_dev, trans, shells)).reshape(pairs, shells)
    energy = ref_norm / sigma
    quadratic = 0.5 * nt(energy, square_wide, precision=highest)
    lane_part = lax.broadcasted_iota(jnp.int32, (part_dev, pairs), 1) // trans
    own = lane_part == lax.broadcasted_iota(jnp.int32, (part_dev, pairs), 0)
    own_wide = jnp.where(own, 1.0, 0.0)
    mask_wide = tn(mask_ref[...].astype(f32), own_wide)
    scores = jnp.where(mask_wide > 0.5, score_ref[...] - quadratic, -1e30)
    top = jnp.max(scores, axis=0, keepdims=True)
    peak = jnp.max(jnp.where(own, jnp.broadcast_to(top, own.shape), -3e38), axis=1, keepdims=True)
    peak_lane = jnp.max(jnp.where(own, jnp.broadcast_to(peak, own.shape), -3e38), axis=0, keepdims=True)
    e = jnp.exp(scores - peak_lane)
    e_ref[...] = e
    total = jnp.sum(
        jnp.where(own, jnp.broadcast_to(jnp.sum(e, axis=0, keepdims=True), own.shape), 0.0), axis=1, keepdims=True
    )

    e_pieces = pieces(e, 2)
    per_row = width // lanes
    for dest in range(dests):
        send_ref[dest, 0:part_dev] = part_ref[:, :, dest * width : (dest + 1) * width]
    half = ori_dev // 2
    for k in range(2):
        piece = e_pieces[k].astype(f32)
        for c in range(half):
            q = k * half + c
            tile = jnp.concatenate([piece[c : c + 1], piece[half + c : half + c + 1]], axis=0).astype(bf16)
            for dest in range(dests):
                send_ref[dest, part_dev + q // per_row, :, (q % per_row) * lanes : (q % per_row + 1) * lanes] = tile

    e_rows = jnp.concatenate([p.astype(f32) for p in e_pieces], axis=0).T.astype(bf16)

    def second_pass(step, carry):
        cols = pl.ds(pl.multiple_of(step * chunk, chunk), chunk)
        wide = jnp.zeros((pairs, chunk), f32)
        for p in range(2):
            plane = planes_ref[p, :, cols]
            mixed = nn(e_rows, jnp.concatenate([plane, plane], axis=0))
            wide = wide + mixed * img_ref[p, :, cols].astype(f32)
        folded = wide.reshape(part_dev, trans // 8, 8, chunk).sum(axis=1).reshape(part_dev * 8, chunk)
        hot = hot_ref[:, cols]
        high, low = pieces(folded, 2)
        return carry + nt(high, hot) + nt(low, hot)

    cross = lax.fori_loop(0, blocks, second_pass, jnp.zeros((part_dev * 8, shells), f32))
    cross = cross.reshape(part_dev, 8, shells).sum(axis=1)
    orient_sums = nt(own_wide, e, precision=highest)
    third = ctf_square * nn(orient_sums, ref_norm, precision=highest)
    noise = part_norm * total - 2.0 * cross + third
    fill = (part_dev, (lanes - shells) // 2)
    stat = jnp.concatenate([noise, jnp.broadcast_to(peak, fill), jnp.broadcast_to(total, fill)], axis=1)
    for dest in range(stat_ref.shape[0]):
        stat_ref[dest] = stat


def column_kernel(
    group_ref,
    recv_ref,
    phase_hbm,
    shell_hbm,
    table_ref,
    img_ref,
    phase_ref,
    shell_ref,
    rows_ref,
    sems,
):
    sources, _, _, width = recv_ref.shape
    part_dev = stat_rows
    trans = phase_ref.shape[0]
    shells = table_ref.shape[1]
    start = pl.multiple_of(lax.axis_index("dom") * width, width)
    phase_copy = pltpu.make_async_copy(phase_hbm.at[:, pl.ds(start, width)], phase_ref, sems.at[0])
    shell_copy = pltpu.make_async_copy(shell_hbm.at[:, pl.ds(start, width)], shell_ref, sems.at[1])
    phase_copy.start()
    shell_copy.start()
    for i in range(sources * part_dev):
        rows_ref[pl.ds(i, 1), :] = table_ref[pl.ds(group_ref[i], 1), :]
    shell_copy.wait()
    phase_copy.wait()
    hot = one_hot(shell_ref[...], shells)
    sine, cosine = sin_cos(phase_ref[...])

    def source_step(src, carry):
        rows = pl.ds(pl.multiple_of(src * part_dev, part_dev), part_dev)
        ctf_pix = sum(nn(p, hot) for p in pieces(rows_ref[rows, :], 3))
        part = recv_ref[src, 0:part_dev].astype(f32)
        row0 = pl.multiple_of(src * part_dev * trans, part_dev * trans)
        write_images(img_ref, row0, 0, part[:, 0, :] * ctf_pix, part[:, 1, :] * ctf_pix, cosine, sine)
        return carry

    lax.fori_loop(0, sources, source_step, 0)


def sum_kernel(
    orients,
    scale,
    group_ref,
    img_ref,
    recv_ref,
    stat_ref,
    e_ref,
    table_ref,
    post_ref,
    sums_ref,
    weights_ref,
    noise_ref,
    half_ref,
    rows_ref,
):
    sources, _, _, width = recv_ref.shape
    part_dev = stat_rows
    ori_dev, pairs = e_ref.shape
    trans = pairs // part_dev
    shells = table_ref.shape[1]
    fill = (lanes - shells) // 2
    me = lax.axis_index("dom")
    mine = lax.axis_index("orient")
    for i in range(sources * part_dev):
        rows_ref[pl.ds(i, 1), :] = table_ref[pl.ds(group_ref[i], 1), :]
    lane_part = lax.broadcasted_iota(jnp.int32, (part_dev, pairs), 1) // trans
    own = lane_part == lax.broadcasted_iota(jnp.int32, (part_dev, pairs), 0)
    per_row = width // lanes
    half = ori_dev // 2

    def factors(src):
        stats = [stat_ref[src * orients + o] for o in range(orients)]
        peaks = [s[:, shells : shells + 1] for s in stats]
        totals = [s[:, shells + fill : shells + fill + 1] for s in stats]
        peak = functools.reduce(jnp.maximum, peaks)
        shares = [jnp.exp(p - peak) for p in peaks]
        total = sum(s * t for s, t in zip(shares, totals))
        inverse = 1.0 / total
        noise = sum(share * stat[:, 0:shells] for share, stat in zip(shares, stats)) * inverse
        my_peak = stat_ref[src * orients + mine][:, shells : shells + 1]
        factor = jnp.exp(my_peak - peak) * inverse
        lane = jnp.sum(jnp.where(own, jnp.broadcast_to(factor, own.shape), 0.0), axis=0, keepdims=True)
        return noise, lane

    def source_step(src, carry):
        noise, weights = carry
        part_noise, lane = factors(src)
        tiles = []
        for k in range(2):
            tops, bottoms = [], []
            for c in range(half):
                q = k * half + c
                col = (q % per_row) * lanes
                tile = recv_ref[src, part_dev + q // per_row, :, col : col + lanes].astype(f32)
                tops.append(tile[0:1])
                bottoms.append(tile[1:2])
            tiles.append(jnp.concatenate(tops + bottoms, axis=0))
        post = (tiles[0] + tiles[1]) * lane
        half_ref[:, pl.ds(pl.multiple_of(src * pairs, pairs), pairs)] = post.astype(bf16)
        rows = rows_ref[pl.ds(pl.multiple_of(src * part_dev, part_dev), part_dev), :]
        per_part = nt(post, jnp.where(own, 1.0, 0.0), precision=highest)
        weights = weights + nn(per_part, rows * rows, precision=highest)
        return noise + part_noise, weights

    noise, weights = lax.fori_loop(
        0, sources, source_step, (jnp.zeros((part_dev, shells), f32), jnp.zeros((ori_dev, shells), f32))
    )
    weights_ref[...] = weights
    noise_ref[...] = jnp.sum(noise, axis=0, keepdims=True) * scale
    _, lane = factors(me)
    post_ref[...] = (e_ref[...] * lane).T
    post_half = half_ref[...]
    for p in range(2):
        sums_ref[:, p, :] = nn(post_half, img_ref[p])


def on_device(particles, references, phases, mask, ctf_group, ctf_table, shell_index, sigma2):
    part_dev, _, pixels = particles.shape
    ori_dev = references.shape[0]
    trans = phases.shape[0]
    groups, shells = ctf_table.shape
    dom = lax.axis_size("dom")
    orients = lax.axis_size("orient")
    width = pixels // dom
    pairs = part_dev * trans
    e_rows = 2 * ori_dev * pairs // (2 * width)
    chunk = 512
    shell_row = shell_index.reshape(1, pixels)
    vmem = pl.BlockSpec(memory_space=pltpu.VMEM)
    smem = pl.BlockSpec(memory_space=pltpu.SMEM)
    anywhere = pl.BlockSpec(memory_space=pl.ANY)
    params = pltpu.CompilerParams(vmem_limit_bytes=vmem_bytes)

    send, stat, e = pl.pallas_call(
        functools.partial(score_kernel, chunk),
        out_shape=(
            jax.ShapeDtypeStruct((dom, part_dev + e_rows, 2, width), bf16),
            jax.ShapeDtypeStruct((dom * orients, stat_rows, lanes), f32),
            jax.ShapeDtypeStruct((ori_dev, pairs), f32),
        ),
        in_specs=[smem] + [vmem] * 7,
        out_specs=(vmem, vmem, vmem),
        scratch_shapes=[
            pltpu.VMEM((2, pairs, pixels), bf16),
            pltpu.VMEM((2, ori_dev, pixels), bf16),
            pltpu.VMEM((shells, pixels), bf16),
            pltpu.VMEM((part_dev, shells), f32),
            pltpu.VMEM((2 * (ori_dev + part_dev), shells), f32),
            pltpu.VMEM((ori_dev, pairs), f32),
        ],
        compiler_params=params,
        name="scores",
    )(ctf_group, particles, references, phases, shell_row, mask, ctf_table, sigma2.reshape(1, shells))

    recv = lax.all_to_all(send, "dom", 0, 0)
    stats = lax.all_to_all(stat, ("dom", "orient"), 0, 0)

    images = pl.pallas_call(
        column_kernel,
        out_shape=jax.ShapeDtypeStruct((2, dom * pairs, width), bf16),
        in_specs=[smem, vmem, anywhere, anywhere, vmem],
        out_specs=vmem,
        scratch_shapes=[
            pltpu.VMEM((trans, width), f32),
            pltpu.VMEM((1, width), jnp.int32),
            pltpu.VMEM((dom * part_dev, shells), f32),
            pltpu.SemaphoreType.DMA((2,)),
        ],
        compiler_params=params,
        name="columns",
    )(ctf_group, recv, phases, shell_row, ctf_table)

    scale = shells / (part_dev * dom * pixels)
    posterior, image_sums, ctf_weights, noise = pl.pallas_call(
        functools.partial(sum_kernel, orients, scale),
        out_shape=(
            jax.ShapeDtypeStruct((pairs, ori_dev), f32),
            jax.ShapeDtypeStruct((ori_dev, 2, width), f32),
            jax.ShapeDtypeStruct((ori_dev, shells), f32),
            jax.ShapeDtypeStruct((1, shells), f32),
        ),
        in_specs=[smem] + [vmem] * 5,
        out_specs=(vmem, vmem, vmem, vmem),
        scratch_shapes=[
            pltpu.VMEM((ori_dev, dom * pairs), bf16),
            pltpu.VMEM((dom * part_dev, shells), f32),
        ],
        compiler_params=params,
        name="sums",
    )(ctf_group, images, recv, stats, e, ctf_table)
    return (
        posterior.reshape(part_dev, trans, ori_dev),
        image_sums,
        ctf_weights,
        noise.reshape(shells),
    )


def solution(mesh):
    return jax.shard_map(
        on_device,
        mesh=mesh,
        in_specs=(
            P("dom", None, None),
            P("orient", None, None),
            P(),
            P("dom", "orient"),
            P(),
            P(),
            P(),
            P(),
        ),
        out_specs=(P("dom", None, "orient"), P("orient", None, "dom"), P("orient", None), P()),
        check_vma=False,
    )
```

time: 174 us -> 59.3 us (0.34)
  blocking collectives: 84.1 us -> 12.6 us
  local copies, waits for them, and re-layouts: 47.1 us -> 13.9 us
  Pallas kernels: 0 us -> 27.4 us
  other arithmetic: 15.6 us -> 0 us
  matrix products: 13.1 us -> 0 us
  loops' own time: 5.91 us -> 0 us
    psum x3 -> x0, blocking collectives: 62.3 us -> none  [the longest x1 39.7 us: on_device(): shell_total = lax.psum(term_one + term_two + term_three, ('dom', 'orient'))]
    pallas_call x0 -> x3, Pallas kernels: none -> 27.4 us  [the longest x1 18.6 us: on_device(): pl.pallas_call(functools.partial(score_kernel, chunk), out_shape=(jax.Sha...]
    dot_general x25 -> x0, matrix products: 13.1 us -> none  [the longest x8 2.67 us: score_block(): jnp.einsum('ptcx,ocx->pto', images, weighted, preferred_element_type=jnp....]
    all_to_all x0 -> x1, blocking collectives: none -> 12.6 us  [on_device(): recv = lax.all_to_all(send, 'dom', 0, 0)]
    pmax x1 -> x0, blocking collectives: 12 us -> none  [on_device(): peak = lax.pmax(local_peak, 'orient')]
    convert_element_type x1 -> x0, local copies, waits for them, and re-layouts: 10.1 us -> none  [on_device(): rows_wide = columns.astype(jnp.float32)]
    all_gather x1 -> x0, blocking collectives: 9.8 us -> none  [on_device(): piece = lax.all_gather(post_half, 'dom', axis=0, tiled=True)]
    convert_element_type x4 -> x0, other arithmetic: 9.48 us -> none  [the longest x1 8.29 us: on_device(): rows_wide = columns.astype(jnp.float32)]
  transfers between devices with their start and end apart: 1 -> 1, of which waited for: 0 -> 0; matrix products, arithmetic and copies ran while one was open for 14% -> 0% of each run, Pallas kernels for 0% -> 6%
where the time goes in v1:
time: 59.3 us; the launch traced here: 58.5 us
  Pallas kernels  27.4 us (46%)
  local copies, waits for them, and re-layouts  13.9 us (23%)
  blocking collectives  12.6 us (21%)
  starting transfers between devices  3.96 us (7%)
  between operations  0.71 us (1%)
    pallas_call x1, Pallas kernels, on_device(): pl.pallas_call(functools.partial(score_kernel, chunk), out_shape=(jax.Sha...  18.6 us
    unnamed x32, local copies, waits for them, and re-layouts  13.9 us
    all_to_all x1, blocking collectives, on_device(): recv = lax.all_to_all(send, 'dom', 0, 0)  12.6 us
    pallas_call x1, Pallas kernels, on_device(): pl.pallas_call(functools.partial(sum_kernel, orients, scale), out_shape=(...  5.42 us
    all_to_all x1, starting transfers between devices, on_device(): stats = lax.all_to_all(stat, ('dom', 'orient'), 0, 0)  3.96 us
    pallas_call x1, Pallas kernels, on_device(): pl.pallas_call(column_kernel, out_shape=jax.ShapeDtypeStruct((2, dom * pa...  3.4 us
  transfers between devices with their start and end apart: 1, of which 0 were waited for; matrix products, arithmetic and copies ran while one was open for 0% of the time, Pallas kernels for 6%

profile of v1, /device:TPU:0, one launch (start us, length us, event | category | flops | bytes accessed | tf_op | source)
XLA Modules:
  0.0 58.5 jit_solution(9730457254824231194)
XLA Ops:
  0.6 0.0 copy-start.13
  0.6 0.0 copy-start.2
  0.7 1.0 %copy-done.2 = f32[16,8192]{1,0:T(8,128)S(1)} copy-done((f32[16,8192]{1,0:T(8,128)S(1)}, f32[16,8192]{1,0:T(8,128)}, u32[]{:S(2)}) %copy-start.2) | copy-done | bytes 524312
  1.7 0.0 copy-start.4
  1.7 1.0 %copy-done.4 = bf16[16,2,8192]{2,1,0:T(2,128)(2,1)S(1)} copy-done((bf16[16,2,8192]{2,1,0:T(2,128)(2,1)S(1)}, bf16[16,2,8192]{2,1,0:T(2,128)(2,1)}, u32[]{:S(2)}) %copy-start.4) | copy-done | bytes 524312
  2.7 0.0 copy-start.5
  2.7 0.8 %copy-done.5 = f32[64,64]{1,0:T(8,128)S(1)} copy-done((f32[64,64]{1,0:T(8,128)S(1)}, f32[64,64]{1,0:T(8,128)}, u32[]{:S(2)}) %copy-start.5) | copy-done | bytes 16408
  3.5 0.0 copy-start.8
  3.5 0.9 %copy-done.8 = bf16[8,2,8192]{2,1,0:T(2,128)(2,1)S(1)} copy-done((bf16[8,2,8192]{2,1,0:T(2,128)(2,1)S(1)}, bf16[8,2,8192]{2,1,0:T(2,128)(2,1)}, u32[]{:S(2)}) %copy-start.8) | copy-done | bytes 262168
  4.4 0.0 copy-start.9
  4.4 0.8 %copy-done.9 = s32[8192]{0:T(1024)S(1)} copy-done((s32[8192]{0:T(1024)S(1)}, s32[8192]{0:T(1024)}, u32[]{:S(2)}) %copy-start.9) | copy-done | bytes 32792
  5.2 0.0 copy-start.11
  5.2 0.7 %copy-done.11 = s32[64]{0:T(128)S(1)} copy-done((s32[64]{0:T(128)S(1)}, s32[64]{0:T(128)}, u32[]{:S(2)}) %copy-start.11) | copy-done | bytes 280
  5.9 0.0 copy-start.14
  5.9 0.7 %copy-done.14 = s32[8,16]{1,0:T(8,128)S(1)} copy-done((s32[8,16]{1,0:T(8,128)S(1)}, s32[8,16]{1,0:T(8,128)}, u32[]{:S(2)}) %copy-start.14) | copy-done | bytes 536
  6.5 0.0 copy-start.15
  6.5 0.7 %copy-done.15 = f32[64]{0:T(128)S(1)} copy-done((f32[64]{0:T(128)S(1)}, f32[64]{0:T(128)}, u32[]{:S(2)}) %copy-start.15) | copy-done | bytes 280
  7.2 0.0 copy-start.7
  7.2 18.6 %scores.1 = (bf16[8,10,2,1024]{3,2,1,0:T(2,128)(2,1)S(1)}, f32[32,8,128]{2,1,0:T(8,128)}, f32[16,128]{1,0:T(8,128)S(1)}) custom-call(s32[64]{0:T(128)S(1)} %copy-done.11, bf16[8,2,8192]{2,1,0:T(2,128)(2,1)S(1)} %copy-done.8, bf16[16,2,8192]{2,1,0:T(2,128)(2,1)S(1)} %copy-done.4, f32[16,8192]{1,0:T(8,128)S(1)} %copy-done.2, s32[1,8192]{1,0:T(1,128)S(1)} %bitcast.4, ...), custom_call_target="tpu_custom_call" | custom-call | tf_op jit(solution)/shard_map/scores/pallas_call | solution.py:336
  25.8 12.6 %all_to_all.10.recv_ref = bf16[8,10,2,1024]{3,2,1,0:T(2,128)(2,1)S(1)} all-to-all(bf16[8,10,2,1024]{3,2,1,0:T(2,128)(2,1)S(1)} %get-tuple-element.11), channel_id=1, replica_groups=mesh['dom'=8,'orient'=4] {'dom'}, dimensions={0} | all-to-all | bytes 655360 | tf_op jit(solution)/shard_map/all_to_all | solution.py:357
  38.4 4.0 %all-to-all-start.1 = ((f32[32,8,128]{2,1,0:T(8,128)}), f32[32,8,128]{2,1,0:T(8,128)S(1)}, u32[]{:S(2)}, u32[]{:S(2)}) async-start(f32[32,8,128]{2,1,0:T(8,128)} %get-tuple-element.12), calls=%async_computation.1 | async-start | bytes 262144 | tf_op jit(solution)/shard_map/all_to_all | solution.py:358
  42.3 0.0 copy-start.3
  42.3 1.0 %copy-done.3 = f32[16,8192]{1,0:T(8,128)S(1)} copy-done((f32[16,8192]{1,0:T(8,128)S(1)}, f32[16,8192]{1,0:T(8,128)}, u32[]{:S(2)}) %copy-start.3) | copy-done | bytes 524312
  43.4 0.0 copy-start.6
  43.4 0.8 %copy-done.6 = f32[64,64]{1,0:T(8,128)S(1)} copy-done((f32[64,64]{1,0:T(8,128)S(1)}, f32[64,64]{1,0:T(8,128)}, u32[]{:S(2)}) %copy-start.6) | copy-done | bytes 16408
  44.1 0.0 copy-start.10
  44.1 0.8 %copy-done.10 = s32[8192]{0:T(1024)S(1)} copy-done((s32[8192]{0:T(1024)S(1)}, s32[8192]{0:T(1024)}, u32[]{:S(2)}) %copy-start.10) | copy-done | bytes 32792
  44.9 0.0 copy-start.12
  44.9 0.7 %copy-done.12 = s32[64]{0:T(128)S(1)} copy-done((s32[64]{0:T(128)S(1)}, s32[64]{0:T(128)}, u32[]{:S(2)}) %copy-start.12) | copy-done | bytes 280
  45.6 3.4 %columns.1.img_ref = bf16[2,1024,1024]{2,1,0:T(8,128)(2,1)S(1)} custom-call(s32[64]{0:T(128)S(1)} %copy-done.12, bf16[8,10,2,1024]{3,2,1,0:T(2,128)(2,1)S(1)} %all_to_all.10.recv_ref, f32[16,8192]{1,0:T(8,128)S(1)} %copy-done.3, s32[1,8192]{1,0:T(1,128)S(1)} %bitcast.5, f32[64,64]{1,0:T(8,128)S(1)} %copy-done.6), custom_call_target="tpu_custom_call" | custom-call | tf_op jit(solution)/shard_map/columns/pallas_call | solution.py:360
  49.0 0.0 copy-start
  49.0 1.9 %copy-done = bf16[2,1024,1024]{2,1,0:T(8,128)(2,1)} copy-done((bf16[2,1024,1024]{2,1,0:T(8,128)(2,1)}, bf16[2,1024,1024]{2,1,0:T(8,128)(2,1)S(1)}, u32[]{:S(2)}) %copy-start) | copy-done | bytes 4194328
  50.9 0.0 all-to-all-done.1.stat_ref
  50.9 0.0 copy-done.13
  50.9 0.0 copy-done.7
  50.9 0.0 copy-start.1
  50.9 2.2 %copy-done.1 = bf16[2,1024,1024]{2,1,0:T(8,128)(2,1)S(1)} copy-done((bf16[2,1024,1024]{2,1,0:T(8,128)(2,1)S(1)}, bf16[2,1024,1024]{2,1,0:T(8,128)(2,1)}, u32[]{:S(2)}) %copy-start.1) | copy-done | bytes 4194328
  53.1 5.4 %sums.1 = (f32[128,16]{1,0:T(8,128)}, f32[16,2,1024]{2,1,0:T(2,128)}, f32[16,64]{1,0:T(8,128)}, f32[1,64]{1,0:T(1,128)}) custom-call(s32[64]{0:T(128)S(1)} %copy-done.13, bf16[2,1024,1024]{2,1,0:T(8,128)(2,1)S(1)} %copy-done.1, bf16[8,10,2,1024]{3,2,1,0:T(2,128)(2,1)S(1)} %all_to_all.10.recv_ref, f32[32,8,128]{2,1,0:T(8,128)S(1)} %all-to-all-done.1.stat_ref, ...), custom_call_target="tpu_custom_call" | custom-call | tf_op jit(solution)/shard_map/sums/pallas_call | solution.py:376
Async XLA Ops:
  0.6 50.3 %copy-start.13 = (s32[64]{0:T(128)S(1)}, s32[64]{0:T(128)}, u32[]{:S(2)}) copy-start(s32[64]{0:T(128)} %group_ref.5) | copy-start | bytes 772
  0.6 1.0 %copy-start.2 = (f32[16,8192]{1,0:T(8,128)S(1)}, f32[16,8192]{1,0:T(8,128)}, u32[]{:S(2)}) copy-start(f32[16,8192]{1,0:T(8,128)} %phase_hbm.1) | copy-start | bytes 1572868
  1.7 1.0 %copy-start.4 = (bf16[16,2,8192]{2,1,0:T(2,128)(2,1)S(1)}, bf16[16,2,8192]{2,1,0:T(2,128)(2,1)}, u32[]{:S(2)}) copy-start(bf16[16,2,8192]{2,1,0:T(2,128)(2,1)} %refs_ref.1) | copy-start | bytes 1572868
  2.7 0.8 %copy-start.5 = (f32[64,64]{1,0:T(8,128)S(1)}, f32[64,64]{1,0:T(8,128)}, u32[]{:S(2)}) copy-start(f32[64,64]{1,0:T(8,128)} %table_ref.5) | copy-start | bytes 49156
  3.5 0.9 %copy-start.8 = (bf16[8,2,8192]{2,1,0:T(2,128)(2,1)S(1)}, bf16[8,2,8192]{2,1,0:T(2,128)(2,1)}, u32[]{:S(2)}) copy-start(bf16[8,2,8192]{2,1,0:T(2,128)(2,1)} %part_ref.1) | copy-start | bytes 786436
  4.4 0.8 %copy-start.9 = (s32[8192]{0:T(1024)S(1)}, s32[8192]{0:T(1024)}, u32[]{:S(2)}) copy-start(s32[8192]{0:T(1024)} %param.14) | copy-start | bytes 98308
  5.2 0.7 %copy-start.11 = (s32[64]{0:T(128)S(1)}, s32[64]{0:T(128)}, u32[]{:S(2)}) copy-start(s32[64]{0:T(128)} %group_ref.5) | copy-start | bytes 772
  5.9 0.7 %copy-start.14 = (s32[8,16]{1,0:T(8,128)S(1)}, s32[8,16]{1,0:T(8,128)}, u32[]{:S(2)}) copy-start(s32[8,16]{1,0:T(8,128)} %mask_ref.1) | copy-start | bytes 1540
  6.5 0.7 %copy-start.15 = (f32[64]{0:T(128)S(1)}, f32[64]{0:T(128)}, u32[]{:S(2)}) copy-start(f32[64]{0:T(128)} %param.15) | copy-start | bytes 772
  7.2 43.7 %copy-start.7 = (f32[64,64]{1,0:T(8,128)S(1)}, f32[64,64]{1,0:T(8,128)}, u32[]{:S(2)}) copy-start(f32[64,64]{1,0:T(8,128)} %table_ref.5) | copy-start | bytes 49156
  38.4 12.6 %all-to-all-start.1 = ((f32[32,8,128]{2,1,0:T(8,128)}), f32[32,8,128]{2,1,0:T(8,128)S(1)}, u32[]{:S(2)}, u32[]{:S(2)}) async-start(f32[32,8,128]{2,1,0:T(8,128)} %get-tuple-element.12), calls=%async_computation.1 | async-start | bytes 262144 | tf_op jit(solution)/shard_map/all_to_all | solution.py:358
  42.3 1.0 %copy-start.3 = (f32[16,8192]{1,0:T(8,128)S(1)}, f32[16,8192]{1,0:T(8,128)}, u32[]{:S(2)}) copy-start(f32[16,8192]{1,0:T(8,128)} %phase_hbm.1) | copy-start | bytes 1572868
  43.4 0.8 %copy-start.6 = (f32[64,64]{1,0:T(8,128)S(1)}, f32[64,64]{1,0:T(8,128)}, u32[]{:S(2)}) copy-start(f32[64,64]{1,0:T(8,128)} %table_ref.5) | copy-start | bytes 49156
  44.1 0.8 %copy-start.10 = (s32[8192]{0:T(1024)S(1)}, s32[8192]{0:T(1024)}, u32[]{:S(2)}) copy-start(s32[8192]{0:T(1024)} %param.14) | copy-start | bytes 98308
  44.9 0.7 %copy-start.12 = (s32[64]{0:T(128)S(1)}, s32[64]{0:T(128)}, u32[]{:S(2)}) copy-start(s32[64]{0:T(128)} %group_ref.5) | copy-start | bytes 772
  49.0 2.0 %copy-start = (bf16[2,1024,1024]{2,1,0:T(8,128)(2,1)}, bf16[2,1024,1024]{2,1,0:T(8,128)(2,1)S(1)}, u32[]{:S(2)}) copy-start(bf16[2,1024,1024]{2,1,0:T(8,128)(2,1)S(1)} %columns.1.img_ref) | copy-start | bytes 12582916
  50.9 2.2 %copy-start.1 = (bf16[2,1024,1024]{2,1,0:T(8,128)(2,1)S(1)}, bf16[2,1024,1024]{2,1,0:T(8,128)(2,1)}, u32[]{:S(2)}) copy-start(bf16[2,1024,1024]{2,1,0:T(8,128)(2,1)} %copy-done) | copy-start | bytes 12582916

commit v2 on v1

v2 whole, which is shorter than its diff:
```python
import functools

import jax
import jax.numpy as jnp
from jax import lax
from jax.experimental import pallas as pl
from jax.experimental.pallas import tpu as pltpu
from jax.sharding import PartitionSpec as P

f32 = jnp.float32
bf16 = jnp.bfloat16
highest = lax.Precision.HIGHEST
vmem_bytes = 60 * 1024 * 1024
lanes = 128

sin_terms = (0.9999999766, -0.1666664762, 0.008332899654, -0.000198008873, 2.590467297e-06)
cos_terms = (0.9999999998, -0.4999999936, 0.04166663624, -0.001388836119, 2.47601506e-05, -2.605130157e-07)


def horner(terms, z):
    total = terms[-1] * z + terms[-2]
    for term in terms[-3::-1]:
        total = total * z + term
    return total


def sin_cos(angle):
    half = angle * 0.5
    z = half * half
    s = half * horner(sin_terms, z)
    c = horner(cos_terms, z)
    twice = s + s
    return twice * c, 1.0 - twice * s


def pieces(x, count):
    out = []
    rest = x
    for step in range(count):
        piece = rest.astype(bf16)
        out.append(piece)
        if step + 1 < count:
            rest = rest - piece.astype(f32)
    return out


def nt(a, b, **kw):
    return lax.dot_general(a, b, (((1,), (1,)), ((), ())), preferred_element_type=f32, **kw)


def tn(a, b, **kw):
    return lax.dot_general(a, b, (((0,), (0,)), ((), ())), preferred_element_type=f32, **kw)


def nn(a, b, **kw):
    return lax.dot_general(a, b, (((1,), (0,)), ((), ())), preferred_element_type=f32, **kw)


def one_hot(index_row, shells):
    rows = lax.broadcasted_iota(jnp.int32, (shells, index_row.shape[1]), 0)
    return jnp.where(rows == index_row, 1.0, 0.0).astype(bf16)


def start_all(pairs, sems):
    copies = [pltpu.make_async_copy(src, dst, sems.at[k]) for k, (src, dst) in enumerate(pairs)]
    for copy in copies:
        copy.start()
    return copies


def split_planes(src, dst_ref, row0):
    items, tiles, load = src
    for tile in range(tiles):
        for item in range(items):
            dst_ref[pl.ds(row0 + (tile * items + item) * 2, 2), :] = load(item, tile).astype(f32)


def read_plane(ref, row0, items, tile, plane):
    return ref[pl.ds(row0 + tile * items * 2 + plane, items, 2), :]


def write_images(store, scaled_ref, scaled_col, cosine, sine, count):
    trans = cosine.shape[0]
    cols = pl.ds(scaled_col, lanes)
    for i in range(count):
        r = jnp.broadcast_to(scaled_ref[i : i + 1, cols], (trans, lanes))
        m = jnp.broadcast_to(scaled_ref[count + i : count + i + 1, cols], (trans, lanes))
        store(0, i, (r * cosine - m * sine).astype(bf16))
        store(1, i, (r * sine + m * cosine).astype(bf16))


def pack_kernel(part_hbm, out_hbm, held_ref, in_sems, out_sems):
    dests, _, _, width = out_hbm.shape
    loads = [
        pltpu.make_async_copy(part_hbm.at[:, :, pl.ds(dest * width, width)], held_ref.at[dest], in_sems.at[dest])
        for dest in range(dests)
    ]
    for load in loads:
        load.start()
    stores = []
    for dest in range(dests):
        loads[dest].wait()
        stores.append(pltpu.make_async_copy(held_ref.at[dest], out_hbm.at[dest], out_sems.at[dest]))
        stores[dest].start()
    for store in stores:
        store.wait()


def score_kernel(
    chunk,
    groups,
    group_ref,
    part_hbm,
    refs_hbm,
    phase_hbm,
    shell_hbm,
    mask_hbm,
    table_hbm,
    sigma_hbm,
    message_ref,
    e_ref,
    part_ref,
    refs_ref,
    phase_ref,
    shell_ref,
    mask_ref,
    table_ref,
    sigma_ref,
    part_rows,
    refs_rows,
    img_ref,
    planes_ref,
    hot_ref,
    scaled_ref,
    rows_ref,
    small_sems,
    big_sems,
):
    part_dev, _, pixels = part_ref.shape
    ori_dev = refs_ref.shape[0]
    trans = phase_ref.shape[0]
    shells = table_ref.shape[1]
    pairs = part_dev * trans
    blocks = pixels // chunk
    tiles = chunk // lanes
    first = lax.axis_index("dom") * part_dev
    small = start_all([(table_hbm, table_ref), (sigma_hbm, sigma_ref), (shell_hbm, shell_ref), (mask_hbm, mask_ref)], small_sems)
    big = []
    for g in range(groups):
        cols = pl.ds(g * (pixels // groups), pixels // groups)
        big.append(
            start_all(
                [
                    (part_hbm.at[:, :, cols], part_ref.at[:, :, cols]),
                    (phase_hbm.at[:, cols], phase_ref.at[:, cols]),
                    (refs_hbm.at[:, :, cols], refs_ref.at[:, :, cols]),
                ],
                big_sems.at[g],
            )
        )
    for copy in small:
        copy.wait()

    for i in range(part_dev):
        rows_ref[pl.ds(i, 1), :] = table_ref[pl.ds(group_ref[first + i], 1), :]
    ctf_rows = rows_ref[...]
    sigma = sigma_ref[...]
    inverse = jnp.broadcast_to(1.0 / sigma, (8, shells))
    table = jnp.concatenate(
        [p.astype(f32) for p in pieces(ctf_rows, 3)] + [p.astype(f32) for p in pieces(inverse, 3)], axis=0
    ).astype(bf16)
    n = part_dev
    norms = None
    scores = None
    for step in range(blocks):
        if step % (blocks // groups) == 0:
            for copy in big[step // (blocks // groups)]:
                copy.wait()
        col0 = step * chunk
        cols = pl.ds(col0, chunk)
        hot = one_hot(shell_ref[:, cols], shells)
        hot_ref[:, cols] = hot
        picked = nn(table, hot)
        ctf_pix = picked[0:n] + picked[n : 2 * n] + picked[2 * n : 3 * n]
        inv_sigma = picked[3 * n : 3 * n + 8] + picked[3 * n + 8 : 3 * n + 16] + picked[3 * n + 16 : 3 * n + 24]
        part0 = step * tiles * part_dev * 2
        refs0 = step * tiles * ori_dev * 2
        split_planes((part_dev, tiles, lambda i, t: part_ref[i, :, pl.ds(col0 + t * lanes, lanes)]), part_rows, part0)
        split_planes((ori_dev, tiles, lambda j, t: refs_ref[j, :, pl.ds(col0 + t * lanes, lanes)]), refs_rows, refs0)
        squares = []
        weighted = [[], []]
        for t in range(tiles):
            here = slice(t * lanes, (t + 1) * lanes)
            tcols = pl.ds(col0 + t * lanes, lanes)
            part_r = read_plane(part_rows, part0, part_dev, t, 0)
            part_m = read_plane(part_rows, part0, part_dev, t, 1)
            refs_r = read_plane(refs_rows, refs0, ori_dev, t, 0)
            refs_m = read_plane(refs_rows, refs0, ori_dev, t, 1)
            ctf = ctf_pix[:, here]
            scaled_ref[0:n, tcols] = part_r * ctf
            scaled_ref[n : 2 * n, tcols] = part_m * ctf
            inv = jnp.concatenate([inv_sigma[:, here]] * (ori_dev // 8), axis=0)
            for p, plane in enumerate((refs_r, refs_m)):
                weighted[p].append((plane * inv).astype(bf16))
                planes_ref[:, pl.ds(2 * col0 + p * chunk + t * lanes, lanes)] = plane.astype(bf16)
            power = jnp.concatenate([refs_r * refs_r + refs_m * refs_m, part_r * part_r + part_m * part_m], axis=0)
            high = power.astype(bf16).astype(f32)
            squares.append(jnp.concatenate([high, power - high], axis=0).astype(bf16))
        more = nt(jnp.concatenate(squares, axis=1), hot)
        norms = more if norms is None else norms + more
        for t in range(tiles):
            sine, cosine = sin_cos(phase_ref[:, pl.ds(col0 + t * lanes, lanes)])

            def store(p, i, value):
                at = 2 * col0 + p * chunk + t * lanes
                img_ref[i * trans : (i + 1) * trans, at : at + lanes] = value

            write_images(store, scaled_ref, col0 + t * lanes, cosine, sine, n)
        more = nt(img_ref[:, 2 * col0 : 2 * (col0 + chunk)], jnp.concatenate(weighted[0] + weighted[1], axis=1))
        scores = more if scores is None else scores + more

    both = ori_dev + part_dev
    norms = norms[0:both, :] + norms[both : 2 * both, :]
    ref_norm = norms[0:ori_dev]
    part_norm = norms[ori_dev:both]
    ctf_square = ctf_rows * ctf_rows
    energy = ref_norm / sigma
    quadratic = 0.5 * nt(ctf_square, energy, precision=highest)
    allowed = jnp.where(mask_ref[...] == 1, 1.0, 0.0)
    wide = (part_dev, trans, ori_dev)
    scores = scores.reshape(wide) - jnp.broadcast_to(quadratic[:, None, :], wide)
    scores = jnp.where(jnp.broadcast_to(allowed[:, None, :], wide) > 0.5, scores, -1e30)
    peak = jnp.max(jnp.max(scores, axis=1, keepdims=True), axis=2, keepdims=True)
    e = jnp.exp(scores - peak)
    orient_sums = jnp.sum(e, axis=1)
    e_wide = e.reshape(pairs, ori_dev)
    e_ref[...] = e_wide
    high = e_wide.astype(bf16)
    e_rows = jnp.concatenate([high.astype(f32), e_wide - high.astype(f32)], axis=1).astype(bf16)

    cross = None
    for step in range(blocks):
        col0 = step * chunk
        plane = planes_ref[:, 2 * col0 : 2 * (col0 + chunk)]
        mixed = nn(e_rows, jnp.concatenate([plane, plane], axis=0))
        total = None
        for p in range(2):
            at = 2 * col0 + p * chunk
            part = mixed[:, p * chunk : (p + 1) * chunk] * img_ref[:, at : at + chunk].astype(f32)
            total = part if total is None else total + part
        folded = total.reshape(part_dev, trans // 8, 8, chunk).sum(axis=1).reshape(part_dev * 8, chunk)
        more = nt(folded.astype(bf16), hot_ref[:, col0 : col0 + chunk])
        cross = more if cross is None else cross + more
    cross = cross.reshape(part_dev, 8, shells).sum(axis=1)
    total = jnp.sum(orient_sums, axis=1, keepdims=True)
    third = ctf_square * nn(orient_sums, ref_norm, precision=highest)
    noise = part_norm * total - 2.0 * cross + third
    lane = lax.broadcasted_iota(jnp.int32, (part_dev, lanes), 1)
    stat = jnp.concatenate([noise, jnp.zeros((part_dev, lanes - shells), f32)], axis=1)
    for k, piece in enumerate(pieces(peak.reshape(part_dev, 1), 3) + pieces(total, 3)):
        stat = jnp.where(lane == shells + k, jnp.broadcast_to(piece.astype(f32), lane.shape), stat)
    message = jnp.concatenate([e_wide.T, stat], axis=0).astype(bf16)

    def spread(dest, carry):
        message_ref[dest] = message
        return carry

    lax.fori_loop(0, message_ref.shape[0], spread, 0, unroll=8)


def column_kernel(
    group_ref,
    recv_hbm,
    phase_hbm,
    shell_hbm,
    table_hbm,
    img_hbm,
    square_hbm,
    recv_ref,
    phase_ref,
    shell_ref,
    table_ref,
    img_ref,
    square_ref,
    rows_ref,
    planes_ref,
    scaled_ref,
    ctf_ref,
    wave_ref,
    sems,
    out_sems,
):
    sources, part_dev, _, width = recv_ref.shape
    trans = phase_ref.shape[0]
    shells = table_ref.shape[1]
    pairs = part_dev * trans
    tiles = width // lanes
    start = pl.multiple_of(lax.axis_index("dom") * width, width)
    copies = start_all(
        [
            (table_hbm, table_ref),
            (shell_hbm.at[:, pl.ds(start, width)], shell_ref),
            (phase_hbm.at[:, pl.ds(start, width)], phase_ref),
            (recv_hbm, recv_ref),
        ],
        sems,
    )
    for copy in copies:
        copy.wait()
    for i in range(sources * part_dev):
        rows_ref[pl.ds(i, 1), :] = table_ref[pl.ds(group_ref[i], 1), :]
    hot = one_hot(shell_ref[...], shells)
    everyone = rows_ref[...]
    ctf_ref[...] = sum(nn(piece, hot) for piece in pieces(everyone, 3))
    square = everyone * everyone
    high = square.astype(bf16).astype(f32)
    squares = jnp.concatenate([high, square - high], axis=1)
    square_ref[...] = (
        jnp.broadcast_to(squares[:, None, :], (sources * part_dev, trans, 2 * shells))
        .reshape(sources * pairs, 2 * shells)
        .astype(bf16)
    )
    square_copy = pltpu.make_async_copy(square_ref, square_hbm, sems.at[0])
    square_copy.start()
    for t in range(tiles):
        cols = pl.ds(t * lanes, lanes)
        sine, cosine = sin_cos(phase_ref[:, cols])
        wave_ref[0:trans, cols] = cosine
        wave_ref[trans : 2 * trans, cols] = sine
    n = part_dev

    def source_step(src, carry):
        plane0 = pl.multiple_of(src * (tiles * part_dev * 2), tiles * part_dev * 2)
        split_planes((part_dev, tiles, lambda i, t: recv_ref[src, i, :, pl.ds(t * lanes, lanes)]), planes_ref, plane0)
        row0 = pl.multiple_of(src * pairs, pairs)
        mine = scaled_ref.at[pl.ds(pl.multiple_of(src * 2 * n, 2 * n), 2 * n), :]
        ctf_here = ctf_ref.at[pl.ds(pl.multiple_of(src * n, n), n), :]
        for t in range(tiles):
            cols = pl.ds(t * lanes, lanes)
            ctf = ctf_here[:, cols]
            mine[0:n, cols] = read_plane(planes_ref, plane0, part_dev, t, 0) * ctf
            mine[n : 2 * n, cols] = read_plane(planes_ref, plane0, part_dev, t, 1) * ctf
        for t in range(tiles):
            cols = pl.ds(t * lanes, lanes)

            def store(p, i, value):
                img_ref[p, pl.ds(row0 + i * trans, trans), cols] = value

            write_images(store, mine, t * lanes, wave_ref[0:trans, cols], wave_ref[trans : 2 * trans, cols], n)
        rows = pl.ds(row0, pairs)
        pltpu.make_async_copy(img_ref.at[:, rows, :], img_hbm.at[:, rows, :], out_sems.at[src]).start()
        return carry

    lax.fori_loop(0, sources, source_step, 0, unroll=2)

    def wait_step(src, carry):
        rows = pl.ds(pl.multiple_of(src * pairs, pairs), pairs)
        pltpu.make_async_copy(img_ref.at[:, rows, :], img_hbm.at[:, rows, :], out_sems.at[src]).wait()
        return carry

    lax.fori_loop(0, sources, wait_step, 0)
    square_copy.wait()


def sum_kernel(
    orients,
    shells,
    scale,
    img_hbm,
    square_hbm,
    recv_hbm,
    e_hbm,
    post_ref,
    sums_ref,
    weights_ref,
    noise_ref,
    img_ref,
    square_ref,
    recv_ref,
    e_ref,
    half_ref,
    share_ref,
    sems,
):
    pairs, ori_dev = e_ref.shape
    part_dev = recv_ref.shape[1] - ori_dev
    trans = pairs // part_dev
    sources = recv_ref.shape[0] // orients
    copies = start_all(
        [(recv_hbm, recv_ref), (e_hbm, e_ref), (square_hbm, square_ref), (img_hbm, img_ref)],
        sems,
    )
    me = lax.axis_index("dom")
    mine = lax.axis_index("orient")
    lane_part = lax.broadcasted_iota(jnp.int32, (part_dev, pairs), 1) // trans
    own = lane_part == lax.broadcasted_iota(jnp.int32, (part_dev, pairs), 0)
    row = lax.broadcasted_iota(jnp.int32, (lanes, 2 * lanes), 0) - shells
    upper = lax.broadcasted_iota(jnp.int32, (lanes, 2 * lanes), 1) // lanes
    picker = jnp.where((row >= 3 * upper) & (row < 3 * upper + 3), 1.0, 0.0).astype(bf16)

    copies[0].wait()
    stats = recv_ref[:, ori_dev : ori_dev + part_dev, :].astype(f32)
    rows = stats.reshape(sources * orients * part_dev, lanes).astype(bf16)
    decoded = nn(rows, picker)
    shape = (sources, orients, part_dev, lanes)
    peaks = decoded[:, 0:lanes].reshape(shape)
    totals = decoded[:, lanes : 2 * lanes].reshape(shape)
    shares = jnp.exp(peaks - jnp.max(peaks, axis=1, keepdims=True))
    shares = shares * (1.0 / jnp.sum(shares * totals, axis=1, keepdims=True))
    noise = jnp.sum(shares * stats.reshape(shape), axis=(0, 1))
    noise_ref[...] = jnp.sum(noise, axis=0, keepdims=True)[:, 0:shells] * scale
    share_ref[...] = shares.reshape(sources * orients, part_dev, lanes)
    for src in range(sources):
        factor = share_ref[src * orients + mine]
        lane = jnp.sum(jnp.where(own, factor, 0.0), axis=0, keepdims=True)
        post = recv_ref[src * orients + mine, 0:ori_dev, :].astype(f32) * lane
        high = post.astype(bf16).astype(f32)
        half_ref[:, pl.ds(src * pairs, pairs)] = jnp.concatenate([high, post - high], axis=0).astype(bf16)
    copies[1].wait()
    factor = share_ref[me * orients + mine][:, 0:ori_dev]
    wide = (part_dev, trans, ori_dev)
    post_ref[...] = (e_ref[...].reshape(wide) * jnp.broadcast_to(factor[:, None, :], wide)).reshape(pairs, ori_dev)
    half = half_ref[...]
    copies[2].wait()
    weights = nn(half, square_ref[...])
    weights = weights[0:ori_dev] + weights[ori_dev : 2 * ori_dev]
    weights_ref[...] = weights[:, 0:shells] + weights[:, shells : 2 * shells]
    copies[3].wait()
    for p in range(2):
        sums = nn(half, img_ref[p])
        sums = sums[0:ori_dev] + sums[ori_dev : 2 * ori_dev]
        for j in range(ori_dev):
            sums_ref[j, p : p + 1, :] = sums[j : j + 1, :]


def on_device(particles, references, phases, mask, ctf_group, ctf_table, shell_index, sigma2):
    part_dev, _, pixels = particles.shape
    ori_dev = references.shape[0]
    trans = phases.shape[0]
    shells = ctf_table.shape[1]
    dom = lax.axis_size("dom")
    orients = lax.axis_size("orient")
    width = pixels // dom
    pairs = part_dev * trans
    chunk = 512
    groups = 4
    shell_row = shell_index.reshape(1, pixels)
    sigma_row = sigma2.reshape(1, shells)
    vmem = pl.BlockSpec(memory_space=pltpu.VMEM)
    smem = pl.BlockSpec(memory_space=pltpu.SMEM)
    anywhere = pl.BlockSpec(memory_space=pl.ANY)
    params = pltpu.CompilerParams(vmem_limit_bytes=vmem_bytes)
    dma = pltpu.SemaphoreType.DMA

    send = pl.pallas_call(
        pack_kernel,
        out_shape=jax.ShapeDtypeStruct((dom, part_dev, 2, width), bf16),
        in_specs=[anywhere],
        out_specs=anywhere,
        scratch_shapes=[pltpu.VMEM((dom, part_dev, 2, width), bf16), dma((dom,)), dma((dom,))],
        compiler_params=params,
        name="pack",
    )(particles)
    recv = lax.all_to_all(send, "dom", 0, 0)

    both = ori_dev + part_dev
    message, e = pl.pallas_call(
        functools.partial(score_kernel, chunk, groups),
        out_shape=(
            jax.ShapeDtypeStruct((dom * orients, both, lanes), bf16),
            jax.ShapeDtypeStruct((pairs, ori_dev), f32),
        ),
        in_specs=[smem] + [anywhere] * 7,
        out_specs=(vmem, vmem),
        scratch_shapes=[
            pltpu.VMEM(particles.shape, bf16),
            pltpu.VMEM(references.shape, bf16),
            pltpu.VMEM(phases.shape, f32),
            pltpu.VMEM((1, pixels), jnp.int32),
            pltpu.VMEM(mask.shape, jnp.int32),
            pltpu.VMEM(ctf_table.shape, f32),
            pltpu.VMEM((1, shells), f32),
            pltpu.VMEM((pixels // lanes * part_dev * 2, lanes), f32),
            pltpu.VMEM((pixels // lanes * ori_dev * 2, lanes), f32),
            pltpu.VMEM((pairs, 2 * pixels), bf16),
            pltpu.VMEM((ori_dev, 2 * pixels), bf16),
            pltpu.VMEM((shells, pixels), bf16),
            pltpu.VMEM((2 * part_dev, pixels), f32),
            pltpu.VMEM((part_dev, shells), f32),
            dma((4,)),
            dma((groups, 3)),
        ],
        compiler_params=params,
        name="scores",
    )(ctf_group, particles, references, phases, shell_row, mask, ctf_table, sigma_row)

    messages = lax.all_to_all(message, ("dom", "orient"), 0, 0)

    images, squares = pl.pallas_call(
        column_kernel,
        out_shape=(
            jax.ShapeDtypeStruct((2, dom * pairs, width), bf16),
            jax.ShapeDtypeStruct((dom * pairs, 2 * shells), bf16),
        ),
        in_specs=[smem] + [anywhere] * 4,
        out_specs=(anywhere, anywhere),
        scratch_shapes=[
            pltpu.VMEM((dom, part_dev, 2, width), bf16),
            pltpu.VMEM((trans, width), f32),
            pltpu.VMEM((1, width), jnp.int32),
            pltpu.VMEM(ctf_table.shape, f32),
            pltpu.VMEM((2, dom * pairs, width), bf16),
            pltpu.VMEM((dom * pairs, 2 * shells), bf16),
            pltpu.VMEM((dom * part_dev, shells), f32),
            pltpu.VMEM((dom * part_dev * 2 * width // lanes, lanes), f32),
            pltpu.VMEM((dom * part_dev * 2, width), f32),
            pltpu.VMEM((dom * part_dev, width), f32),
            pltpu.VMEM((2 * trans, width), f32),
            dma((4,)),
            dma((dom,)),
        ],
        compiler_params=params,
        name="columns",
    )(ctf_group, recv, phases, shell_row, ctf_table)

    scale = shells / (part_dev * dom * pixels)
    posterior, image_sums, ctf_weights, noise = pl.pallas_call(
        functools.partial(sum_kernel, orients, shells, scale),
        out_shape=(
            jax.ShapeDtypeStruct((pairs, ori_dev), f32),
            jax.ShapeDtypeStruct((ori_dev, 2, width), f32),
            jax.ShapeDtypeStruct((ori_dev, shells), f32),
            jax.ShapeDtypeStruct((1, shells), f32),
        ),
        in_specs=[anywhere] * 4,
        out_specs=(vmem, vmem, vmem, vmem),
        scratch_shapes=[
            pltpu.VMEM((2, dom * pairs, width), bf16),
            pltpu.VMEM((dom * pairs, 2 * shells), bf16),
            pltpu.VMEM((dom * orients, both, lanes), bf16),
            pltpu.VMEM((pairs, ori_dev), f32),
            pltpu.VMEM((2 * ori_dev, dom * pairs), bf16),
            pltpu.VMEM((dom * orients, part_dev, lanes), f32),
            dma((4,)),
        ],
        compiler_params=params,
        name="sums",
    )(images, squares, messages, e)
    return (
        posterior.reshape(part_dev, trans, ori_dev),
        image_sums,
        ctf_weights,
        noise.reshape(shells),
    )


def solution(mesh):
    return jax.shard_map(
        on_device,
        mesh=mesh,
        in_specs=(
            P("dom", None, None),
            P("orient", None, None),
            P(),
            P("dom", "orient"),
            P(),
            P(),
            P(),
            P(),
        ),
        out_specs=(P("dom", None, "orient"), P("orient", None, "dom"), P("orient", None), P()),
        check_vma=False,
    )
```

time: 59.3 us -> 38.4 us (0.65)
  local copies, waits for them, and re-layouts: 13.9 us -> 0.7 us
  blocking collectives: 12.6 us -> 0 us
  starting transfers between devices: 3.96 us -> 11.5 us
  Pallas kernels: 27.4 us -> 20.2 us
  waiting for transfers between devices: 0.01 us -> 4.84 us
    unnamed x32 -> x4, local copies, waits for them, and re-layouts: 13.9 us -> 0.7 us
    all_to_all x1 -> x0, blocking collectives: 12.6 us -> none  [on_device(): recv = lax.all_to_all(send, 'dom', 0, 0)]
    all_to_all x1 -> x2, starting transfers between devices: 3.96 us -> 11.5 us  [the longest x1 6.33 us: on_device(): messages = lax.all_to_all(message, ('dom', 'orient'), 0, 0)]
    pallas_call x3 -> x4, Pallas kernels: 27.4 us -> 20.2 us  [the longest x1 10.2 us: on_device(): pl.pallas_call(functools.partial(score_kernel, chunk, groups), out_shape=...]
    all_to_all x1 -> x2, waiting for transfers between devices: 0.01 us -> 4.84 us  [the longest x1 4.83 us: on_device(): messages = lax.all_to_all(message, ('dom', 'orient'), 0, 0)]
  transfers between devices with their start and end apart: 1 -> 2, of which waited for: 0 -> 1; matrix products, arithmetic and copies ran while one was open for 0% -> 0% of each run, Pallas kernels for 6% -> 39%
where the time goes in v2:
time: 38.4 us; the launch traced here: 37.9 us
  Pallas kernels  20.2 us (53%)
  starting transfers between devices  11.5 us (30%)
  waiting for transfers between devices  4.84 us (13%)
  local copies, waits for them, and re-layouts  0.7 us (2%)
  between operations  0.69 us (2%)
    pallas_call x1, Pallas kernels, on_device(): pl.pallas_call(functools.partial(score_kernel, chunk, groups), out_shape=...  10.2 us
    all_to_all x1, starting transfers between devices, on_device(): messages = lax.all_to_all(message, ('dom', 'orient'), 0, 0)  6.33 us
    all_to_all x1, starting transfers between devices, on_device(): recv = lax.all_to_all(send, 'dom', 0, 0)  5.18 us
    all_to_all x1, waiting for transfers between devices, on_device(): messages = lax.all_to_all(message, ('dom', 'orient'), 0, 0)  4.83 us
    pallas_call x1, Pallas kernels, on_device(): pl.pallas_call(column_kernel, out_shape=(jax.ShapeDtypeStruct((2, dom * p...  4.48 us
    pallas_call x1, Pallas kernels, on_device(): pl.pallas_call(functools.partial(sum_kernel, orients, shells, scale), out...  3.91 us
    pallas_call x1, Pallas kernels, on_device(): pl.pallas_call(pack_kernel, out_shape=jax.ShapeDtypeStruct((dom, part_dev...  1.63 us
  transfers between devices with their start and end apart: 2, of which 1 were waited for; matrix products, arithmetic and copies ran while one was open for 0% of the time, Pallas kernels for 39%

profile of v2, /device:TPU:0, one launch (start us, length us, event | category | flops | bytes accessed | tf_op | source)
XLA Modules:
  0.0 37.9 jit_solution(12390454332421598680)
XLA Ops:
  0.6 1.6 %pack.1 = bf16[8,8,2,1024]{3,2,1,0:T(2,128)(2,1)} custom-call(bf16[8,2,8192]{2,1,0:T(2,128)(2,1)} %part_hbm.3), custom_call_target="tpu_custom_call" | custom-call | tf_op jit(solution)/shard_map/pack/pallas_call | solution.py:455
  2.3 5.2 %all-to-all-start = ((bf16[8,8,2,1024]{3,2,1,0:T(2,128)(2,1)}), bf16[8,8,2,1024]{3,2,1,0:T(2,128)(2,1)S(1)}, u32[]{:S(2)}, u32[]{:S(2)}) async-start(bf16[8,8,2,1024]{3,2,1,0:T(2,128)(2,1)} %pack.1), calls=%async_computation | async-start | bytes 524288 | tf_op jit(solution)/shard_map/all_to_all | solution.py:464
  7.4 10.2 %scores.1 = (bf16[32,24,128]{2,1,0:T(8,128)(2,1)}, f32[128,16]{1,0:T(8,128)}) custom-call(s32[64]{0:T(128)} %group_ref.3, bf16[8,2,8192]{2,1,0:T(2,128)(2,1)} %part_hbm.3, bf16[16,2,8192]{2,1,0:T(2,128)(2,1)} %refs_hbm.1, f32[16,8192]{1,0:T(8,128)} %phase_hbm.3, s32[1,8192]{1,0:T(1,128)} %bitcast.4, s32[8,16]{1,0:T(8,128)} %mask_hbm.1, f32[64,64]{1,0:T(8,128)} %table_hbm.3, ...), custom_call_target="tpu_custom_call" | custom-call | tf_op jit(solution)/shard_map/scores/pallas_call | solution.py:467
  17.7 0.0 all-to-all-done.recv_hbm
  17.7 0.0 copy-start
  17.7 6.3 %all-to-all-start.1 = ((bf16[32,24,128]{2,1,0:T(8,128)(2,1)}), bf16[32,24,128]{2,1,0:T(8,128)(2,1)S(1)}, u32[]{:S(2)}, u32[]{:S(2)}) async-start(bf16[32,24,128]{2,1,0:T(8,128)(2,1)} %get-tuple-element.14), calls=%async_computation.1 | async-start | bytes 393216 | tf_op jit(solution)/shard_map/all_to_all | solution.py:497
  24.0 0.0 copy-done
  24.0 4.5 %columns.1 = (bf16[2,1024,1024]{2,1,0:T(8,128)(2,1)}, bf16[1024,128]{1,0:T(8,128)(2,1)}) custom-call(s32[64]{0:T(128)} %group_ref.3, bf16[8,8,2,1024]{3,2,1,0:T(2,128)(2,1)} %copy-done, f32[16,8192]{1,0:T(8,128)} %phase_hbm.3, s32[1,8192]{1,0:T(1,128)} %bitcast.5, f32[64,64]{1,0:T(8,128)} %table_hbm.3), custom_call_target="tpu_custom_call" | custom-call | tf_op jit(solution)/shard_map/columns/pallas_call | solution.py:499
  28.5 4.8 %all-to-all-done.1.recv_hbm = bf16[32,24,128]{2,1,0:T(8,128)(2,1)S(1)} async-done(((bf16[32,24,128]{2,1,0:T(8,128)(2,1)}), bf16[32,24,128]{2,1,0:T(8,128)(2,1)S(1)}, u32[]{:S(2)}, u32[]{:S(2)}) %all-to-all-start.1) | async-done | bytes 196640 | tf_op jit(solution)/shard_map/all_to_all | solution.py:497
  33.3 0.0 copy-start.1
  33.3 0.7 %copy-done.1 = bf16[32,24,128]{2,1,0:T(8,128)(2,1)} copy-done((bf16[32,24,128]{2,1,0:T(8,128)(2,1)}, bf16[32,24,128]{2,1,0:T(8,128)(2,1)S(1)}, u32[]{:S(2)}) %copy-start.1) | copy-done | bytes 196632
  34.0 3.9 %sums.1 = (f32[128,16]{1,0:T(8,128)}, f32[16,2,1024]{2,1,0:T(2,128)}, f32[16,64]{1,0:T(8,128)}, f32[1,64]{1,0:T(1,128)}) custom-call(bf16[2,1024,1024]{2,1,0:T(8,128)(2,1)} %get-tuple-element.12.img_hbm, bf16[1024,128]{1,0:T(8,128)(2,1)} %get-tuple-element.13.square_hbm, bf16[32,24,128]{2,1,0:T(8,128)(2,1)} %copy-done.1, f32[128,16]{1,0:T(8,128)} %get-tuple-element.15.e_hbm), custom_call_target="tpu_custom_call" | custom-call | tf_op jit(solution)/shard_map/sums/pallas_call | solution.py:527
Async XLA Ops:
  2.3 15.4 %all-to-all-start = ((bf16[8,8,2,1024]{3,2,1,0:T(2,128)(2,1)}), bf16[8,8,2,1024]{3,2,1,0:T(2,128)(2,1)S(1)}, u32[]{:S(2)}, u32[]{:S(2)}) async-start(bf16[8,8,2,1024]{3,2,1,0:T(2,128)(2,1)} %pack.1), calls=%async_computation | async-start | bytes 524288 | tf_op jit(solution)/shard_map/all_to_all | solution.py:464
  17.7 6.3 %copy-start = (bf16[8,8,2,1024]{3,2,1,0:T(2,128)(2,1)}, bf16[8,8,2,1024]{3,2,1,0:T(2,128)(2,1)S(1)}, u32[]{:S(2)}) copy-start(bf16[8,8,2,1024]{3,2,1,0:T(2,128)(2,1)S(1)} %all-to-all-done.recv_hbm) | copy-start | bytes 786436
  17.7 15.7 %all-to-all-start.1 = ((bf16[32,24,128]{2,1,0:T(8,128)(2,1)}), bf16[32,24,128]{2,1,0:T(8,128)(2,1)S(1)}, u32[]{:S(2)}, u32[]{:S(2)}) async-start(bf16[32,24,128]{2,1,0:T(8,128)(2,1)} %get-tuple-element.14), calls=%async_computation.1 | async-start | bytes 393216 | tf_op jit(solution)/shard_map/all_to_all | solution.py:497
  33.3 0.7 %copy-start.1 = (bf16[32,24,128]{2,1,0:T(8,128)(2,1)}, bf16[32,24,128]{2,1,0:T(8,128)(2,1)S(1)}, u32[]{:S(2)}) copy-start(bf16[32,24,128]{2,1,0:T(8,128)(2,1)S(1)} %all-to-all-done.1.recv_hbm) | copy-start | bytes 589828

commit v3 on v2

--- a/solution.py
+++ b/solution.py
@@ -10,8 +10,8 @@
 f32 = jnp.float32
 bf16 = jnp.bfloat16
 highest = lax.Precision.HIGHEST
-vmem_bytes = 60 * 1024 * 1024
 lanes = 128
+wave_tile = 256
 
 sin_terms = (0.9999999766, -0.1666664762, 0.008332899654, -0.000198008873, 2.590467297e-06)
 cos_terms = (0.9999999998, -0.4999999936, 0.04166663624, -0.001388836119, 2.47601506e-05, -2.605130157e-07)
@@ -89,27 +89,19 @@
         store(1, i, (r * sine + m * cosine).astype(bf16))
 
 
-def pack_kernel(part_hbm, out_hbm, held_ref, in_sems, out_sems):
-    dests, _, _, width = out_hbm.shape
-    loads = [
-        pltpu.make_async_copy(part_hbm.at[:, :, pl.ds(dest * width, width)], held_ref.at[dest], in_sems.at[dest])
-        for dest in range(dests)
-    ]
-    for load in loads:
-        load.start()
-    stores = []
-    for dest in range(dests):
-        loads[dest].wait()
-        stores.append(pltpu.make_async_copy(held_ref.at[dest], out_hbm.at[dest], out_sems.at[dest]))
-        stores[dest].start()
-    for store in stores:
-        store.wait()
+def pack_kernel(part_hbm, out_ref, sems):
+    dests, _, _, width = out_ref.shape
+    copies = start_all(
+        [(part_hbm.at[:, :, pl.ds(dest * width, width)], out_ref.at[dest]) for dest in range(dests)], sems
+    )
+    for copy in copies:
+        copy.wait()
 
 
 def score_kernel(
     chunk,
     groups,
-    group_ref,
+    group_hbm,
     part_hbm,
     refs_hbm,
     phase_hbm,
@@ -126,6 +118,7 @@
     mask_ref,
     table_ref,
     sigma_ref,
+    group_ref,
     part_rows,
     refs_rows,
     img_ref,
@@ -144,7 +137,16 @@
     blocks = pixels // chunk
     tiles = chunk // lanes
     first = lax.axis_index("dom") * part_dev
-    small = start_all([(table_hbm, table_ref), (sigma_hbm, sigma_ref), (shell_hbm, shell_ref), (mask_hbm, mask_ref)], small_sems)
+    small = start_all(
+        [
+            (group_hbm, group_ref),
+            (table_hbm, table_ref),
+            (sigma_hbm, sigma_ref),
+            (shell_hbm, shell_ref),
+            (mask_hbm, mask_ref),
+        ],
+        small_sems,
+    )
     big = []
     for g in range(groups):
         cols = pl.ds(g * (pixels // groups), pixels // groups)
@@ -269,39 +271,39 @@
 
 
 def column_kernel(
-    group_ref,
-    recv_hbm,
+    group_hbm,
+    recv_ref,
     phase_hbm,
     shell_hbm,
     table_hbm,
-    img_hbm,
+    scaled_hbm,
+    wave_hbm,
     square_hbm,
-    recv_ref,
+    group_ref,
     phase_ref,
     shell_ref,
     table_ref,
-    img_ref,
+    scaled_ref,
+    wave_ref,
     square_ref,
     rows_ref,
     planes_ref,
-    scaled_ref,
     ctf_ref,
-    wave_ref,
     sems,
-    out_sems,
 ):
     sources, part_dev, _, width = recv_ref.shape
     trans = phase_ref.shape[0]
     shells = table_ref.shape[1]
     pairs = part_dev * trans
     tiles = width // lanes
+    span = wave_tile // lanes
     start = pl.multiple_of(lax.axis_index("dom") * width, width)
     copies = start_all(
         [
+            (group_hbm, group_ref),
             (table_hbm, table_ref),
             (shell_hbm.at[:, pl.ds(start, width)], shell_ref),
             (phase_hbm.at[:, pl.ds(start, width)], phase_ref),
-            (recv_hbm, recv_ref),
         ],
         sems,
     )
@@ -312,6 +314,13 @@
     hot = one_hot(shell_ref[...], shells)
     everyone = rows_ref[...]
     ctf_ref[...] = sum(nn(piece, hot) for piece in pieces(everyone, 3))
+    for t in range(tiles):
+        at = (t // span * 2 * span + t % span) * lanes
+        sine, cosine = sin_cos(phase_ref[:, pl.ds(t * lanes, lanes)])
+        for wave, offset in ((cosine, at), (sine, at + wave_tile)):
+            high = wave.astype(bf16)
+            wave_ref[0:trans, pl.ds(offset, lanes)] = high
+            wave_ref[trans : 2 * trans, pl.ds(offset, lanes)] = (wave - high.astype(f32)).astype(bf16)
     square = everyone * everyone
     high = square.astype(bf16).astype(f32)
     squares = jnp.concatenate([high, square - high], axis=1)
@@ -320,65 +329,43 @@
         .reshape(sources * pairs, 2 * shells)
         .astype(bf16)
     )
-    square_copy = pltpu.make_async_copy(square_ref, square_hbm, sems.at[0])
-    square_copy.start()
-    for t in range(tiles):
-        cols = pl.ds(t * lanes, lanes)
-        sine, cosine = sin_cos(phase_ref[:, cols])
-        wave_ref[0:trans, cols] = cosine
-        wave_ref[trans : 2 * trans, cols] = sine
     n = part_dev
 
     def source_step(src, carry):
         plane0 = pl.multiple_of(src * (tiles * part_dev * 2), tiles * part_dev * 2)
         split_planes((part_dev, tiles, lambda i, t: recv_ref[src, i, :, pl.ds(t * lanes, lanes)]), planes_ref, plane0)
-        row0 = pl.multiple_of(src * pairs, pairs)
-        mine = scaled_ref.at[pl.ds(pl.multiple_of(src * 2 * n, 2 * n), 2 * n), :]
-        ctf_here = ctf_ref.at[pl.ds(pl.multiple_of(src * n, n), n), :]
+        rows = pl.ds(pl.multiple_of(src * n, n), n)
         for t in range(tiles):
             cols = pl.ds(t * lanes, lanes)
-            ctf = ctf_here[:, cols]
-            mine[0:n, cols] = read_plane(planes_ref, plane0, part_dev, t, 0) * ctf
-            mine[n : 2 * n, cols] = read_plane(planes_ref, plane0, part_dev, t, 1) * ctf
-        for t in range(tiles):
-            cols = pl.ds(t * lanes, lanes)
-
-            def store(p, i, value):
-                img_ref[p, pl.ds(row0 + i * trans, trans), cols] = value
-
-            write_images(store, mine, t * lanes, wave_ref[0:trans, cols], wave_ref[trans : 2 * trans, cols], n)
-        rows = pl.ds(row0, pairs)
-        pltpu.make_async_copy(img_ref.at[:, rows, :], img_hbm.at[:, rows, :], out_sems.at[src]).start()
+            ctf = ctf_ref[rows, cols]
+            for p in range(2):
+                scaled_ref[p, rows, cols] = read_plane(planes_ref, plane0, part_dev, t, p) * ctf
         return carry
 
     lax.fori_loop(0, sources, source_step, 0, unroll=2)
-
-    def wait_step(src, carry):
-        rows = pl.ds(pl.multiple_of(src * pairs, pairs), pairs)
-        pltpu.make_async_copy(img_ref.at[:, rows, :], img_hbm.at[:, rows, :], out_sems.at[src]).wait()
-        return carry
-
-    lax.fori_loop(0, sources, wait_step, 0)
-    square_copy.wait()
+    copies = start_all([(scaled_ref, scaled_hbm), (wave_ref, wave_hbm), (square_ref, square_hbm)], sems)
+    for copy in copies:
+        copy.wait()
 
 
 def sum_kernel(
     orients,
     shells,
     scale,
-    img_hbm,
+    scaled_hbm,
+    wave_hbm,
     square_hbm,
-    recv_hbm,
-    e_hbm,
+    recv_ref,
+    e_ref,
     post_ref,
     sums_ref,
     weights_ref,
     noise_ref,
-    img_ref,
+    scaled_ref,
+    wave_ref,
     square_ref,
-    recv_ref,
-    e_ref,
     half_ref,
+    left_ref,
     share_ref,
     sems,
 ):
@@ -386,19 +373,18 @@
     part_dev = recv_ref.shape[1] - ori_dev
     trans = pairs // part_dev
     sources = recv_ref.shape[0] // orients
-    copies = start_all(
-        [(recv_hbm, recv_ref), (e_hbm, e_ref), (square_hbm, square_ref), (img_hbm, img_ref)],
-        sems,
-    )
+    copies = start_all([(wave_hbm, wave_ref), (scaled_hbm, scaled_ref), (square_hbm, square_ref)], sems)
     me = lax.axis_index("dom")
     mine = lax.axis_index("orient")
     lane_part = lax.broadcasted_iota(jnp.int32, (part_dev, pairs), 1) // trans
     own = lane_part == lax.broadcasted_iota(jnp.int32, (part_dev, pairs), 0)
+    lane = lax.broadcasted_iota(jnp.int32, (ori_dev, pairs), 1)
+    lower = lane < pairs // 2
+    half_part = lane % (pairs // 2) // trans
     row = lax.broadcasted_iota(jnp.int32, (lanes, 2 * lanes), 0) - shells
     upper = lax.broadcasted_iota(jnp.int32, (lanes, 2 * lanes), 1) // lanes
     picker = jnp.where((row >= 3 * upper) & (row < 3 * upper + 3), 1.0, 0.0).astype(bf16)
 
-    copies[0].wait()
     stats = recv_ref[:, ori_dev : ori_dev + part_dev, :].astype(f32)
     rows = stats.reshape(sources * orients * part_dev, lanes).astype(bf16)
     decoded = nn(rows, picker)
@@ -415,22 +401,44 @@
         lane = jnp.sum(jnp.where(own, factor, 0.0), axis=0, keepdims=True)
         post = recv_ref[src * orients + mine, 0:ori_dev, :].astype(f32) * lane
         high = post.astype(bf16).astype(f32)
-        half_ref[:, pl.ds(src * pairs, pairs)] = jnp.concatenate([high, post - high], axis=0).astype(bf16)
-    copies[1].wait()
+        low = post - high
+        half_ref[:, pl.ds(src * pairs, pairs)] = jnp.concatenate([high, low], axis=0).astype(bf16)
+        turned = [pltpu.roll(x, pairs // 2, 1) for x in (high, low)]
+        mixes = (jnp.where(lower, high, turned[1]), jnp.where(lower, turned[0], low))
+        highs = (high, turned[0])
+        for i in range(part_dev):
+            rows = pl.ds((src * part_dev + i) * ori_dev, ori_dev)
+            group = i // (part_dev // 2)
+            here = half_part == i % (part_dev // 2)
+            left_ref[rows, 0:pairs] = jnp.where(here, mixes[group], 0.0).astype(bf16)
+            left_ref[rows, pairs : 2 * pairs] = jnp.where(here & lower, highs[group], 0.0).astype(bf16)
     factor = share_ref[me * orients + mine][:, 0:ori_dev]
     wide = (part_dev, trans, ori_dev)
     post_ref[...] = (e_ref[...].reshape(wide) * jnp.broadcast_to(factor[:, None, :], wide)).reshape(pairs, ori_dev)
-    half = half_ref[...]
+    copies[0].wait()
+    copies[1].wait()
+    for tile in range(sums_ref.shape[2] // wave_tile):
+        cols = slice(tile * wave_tile, (tile + 1) * wave_tile)
+        waves = wave_ref[:, 2 * tile * wave_tile : 2 * (tile + 1) * wave_tile]
+        high = waves[0:trans]
+        low = waves[trans : 2 * trans]
+        mixed = nn(left_ref[...], jnp.concatenate([high] * part_dev + [low] * part_dev, axis=0))
+        sums = [None, None]
+        for i in range(sources * part_dev):
+            block = mixed[i * ori_dev : (i + 1) * ori_dev]
+            cosine = block[:, 0:wave_tile]
+            sine = block[:, wave_tile : 2 * wave_tile]
+            r = jnp.broadcast_to(scaled_ref[0, i : i + 1, cols], cosine.shape)
+            m = jnp.broadcast_to(scaled_ref[1, i : i + 1, cols], cosine.shape)
+            more = (r * cosine - m * sine, r * sine + m * cosine)
+            sums = [new if old is None else old + new for old, new in zip(sums, more)]
+        for p in range(2):
+            for j in range(ori_dev):
+                sums_ref[j, p : p + 1, cols] = sums[p][j : j + 1, :]
     copies[2].wait()
-    weights = nn(half, square_ref[...])
+    weights = nn(half_ref[...], square_ref[...])
     weights = weights[0:ori_dev] + weights[ori_dev : 2 * ori_dev]
     weights_ref[...] = weights[:, 0:shells] + weights[:, shells : 2 * shells]
-    copies[3].wait()
-    for p in range(2):
-        sums = nn(half, img_ref[p])
-        sums = sums[0:ori_dev] + sums[ori_dev : 2 * ori_dev]
-        for j in range(ori_dev):
-            sums_ref[j, p : p + 1, :] = sums[j : j + 1, :]
 
 
 def on_device(particles, references, phases, mask, ctf_group, ctf_table, shell_index, sigma2):
@@ -442,25 +450,26 @@
     orients = lax.axis_size("orient")
     width = pixels // dom
     pairs = part_dev * trans
-    chunk = 512
-    groups = 4
+    chunk = 2048
+    groups = 1
     shell_row = shell_index.reshape(1, pixels)
     sigma_row = sigma2.reshape(1, shells)
     vmem = pl.BlockSpec(memory_space=pltpu.VMEM)
     smem = pl.BlockSpec(memory_space=pltpu.SMEM)
     anywhere = pl.BlockSpec(memory_space=pl.ANY)
-    params = pltpu.CompilerParams(vmem_limit_bytes=vmem_bytes)
+    params = pltpu.CompilerParams(vmem_limit_bytes=20 * 1024 * 1024)
+    far = lambda x: pltpu.with_memory_space_constraint(x, pltpu.HBM)
     dma = pltpu.SemaphoreType.DMA
 
     send = pl.pallas_call(
         pack_kernel,
-        out_shape=jax.ShapeDtypeStruct((dom, part_dev, 2, width), bf16),
+        out_shape=pltpu.VMEM((dom, part_dev, 2, width), bf16),
         in_specs=[anywhere],
-        out_specs=anywhere,
-        scratch_shapes=[pltpu.VMEM((dom, part_dev, 2, width), bf16), dma((dom,)), dma((dom,))],
+        out_specs=vmem,
+        scratch_shapes=[dma((dom,))],
         compiler_params=params,
         name="pack",
-    )(particles)
+    )(far(particles))
     recv = lax.all_to_all(send, "dom", 0, 0)
 
     both = ori_dev + part_dev
@@ -470,7 +479,7 @@
             jax.ShapeDtypeStruct((dom * orients, both, lanes), bf16),
             jax.ShapeDtypeStruct((pairs, ori_dev), f32),
         ),
-        in_specs=[smem] + [anywhere] * 7,
+        in_specs=[anywhere] * 8,
         out_specs=(vmem, vmem),
         scratch_shapes=[
             pltpu.VMEM(particles.shape, bf16),
@@ -480,6 +489,7 @@
             pltpu.VMEM(mask.shape, jnp.int32),
             pltpu.VMEM(ctf_table.shape, f32),
             pltpu.VMEM((1, shells), f32),
+            pltpu.SMEM(ctf_group.shape, jnp.int32),
             pltpu.VMEM((pixels // lanes * part_dev * 2, lanes), f32),
             pltpu.VMEM((pixels // lanes * ori_dev * 2, lanes), f32),
             pltpu.VMEM((pairs, 2 * pixels), bf16),
@@ -487,41 +497,51 @@
             pltpu.VMEM((shells, pixels), bf16),
             pltpu.VMEM((2 * part_dev, pixels), f32),
             pltpu.VMEM((part_dev, shells), f32),
-            dma((4,)),
+            dma((5,)),
             dma((groups, 3)),
         ],
         compiler_params=params,
         name="scores",
-    )(ctf_group, particles, references, phases, shell_row, mask, ctf_table, sigma_row)
+    )(
+        far(ctf_group),
+        far(particles),
+        far(references),
+        far(phases),
+        far(shell_row),
+        far(mask),
+        far(ctf_table),
+        far(sigma_row),
+    )
 
     messages = lax.all_to_all(message, ("dom", "orient"), 0, 0)
 
-    images, squares = pl.pallas_call(
+    particles_all = dom * part_dev
+    columns = (
+        ((2, particles_all, width), f32),
+        ((2 * trans, 2 * width), bf16),
+        ((particles_all * trans, 2 * shells), bf16),
+    )
+    scaled, waves, squares = pl.pallas_call(
         column_kernel,
-        out_shape=(
-            jax.ShapeDtypeStruct((2, dom * pairs, width), bf16),
-            jax.ShapeDtypeStruct((dom * pairs, 2 * shells), bf16),
-        ),
-        in_specs=[smem] + [anywhere] * 4,
-        out_specs=(anywhere, anywhere),
+        out_shape=tuple(pltpu.HBM(*column) for column in columns),
+        in_specs=[anywhere, vmem] + [anywhere] * 3,
+        out_specs=(anywhere,) * 3,
         scratch_shapes=[
-            pltpu.VMEM((dom, part_dev, 2, width), bf16),
+            pltpu.SMEM(ctf_group.shape, jnp.int32),
             pltpu.VMEM((trans, width), f32),
             pltpu.VMEM((1, width), jnp.int32),
             pltpu.VMEM(ctf_table.shape, f32),
-            pltpu.VMEM((2, dom * pairs, width), bf16),
-            pltpu.VMEM((dom * pairs, 2 * shells), bf16),
-            pltpu.VMEM((dom * part_dev, shells), f32),
-            pltpu.VMEM((dom * part_dev * 2 * width // lanes, lanes), f32),
-            pltpu.VMEM((dom * part_dev * 2, width), f32),
-            pltpu.VMEM((dom * part_dev, width), f32),
-            pltpu.VMEM((2 * trans, width), f32),
+        ]
+        + [pltpu.VMEM(*column) for column in columns]
+        + [
+            pltpu.VMEM((particles_all, shells), f32),
+            pltpu.VMEM((particles_all * 2 * width // lanes, lanes), f32),
+            pltpu.VMEM((particles_all, width), f32),
             dma((4,)),
-            dma((dom,)),
         ],
         compiler_params=params,
         name="columns",
-    )(ctf_group, recv, phases, shell_row, ctf_table)
+    )(far(ctf_group), recv, far(phases), far(shell_row), far(ctf_table))
 
     scale = shells / (part_dev * dom * pixels)
     posterior, image_sums, ctf_weights, noise = pl.pallas_call(
@@ -532,20 +552,18 @@
             jax.ShapeDtypeStruct((ori_dev, shells), f32),
             jax.ShapeDtypeStruct((1, shells), f32),
         ),
-        in_specs=[anywhere] * 4,
+        in_specs=[anywhere, anywhere, anywhere, vmem, vmem],
         out_specs=(vmem, vmem, vmem, vmem),
-        scratch_shapes=[
-            pltpu.VMEM((2, dom * pairs, width), bf16),
-            pltpu.VMEM((dom * pairs, 2 * shells), bf16),
-            pltpu.VMEM((dom * orients, both, lanes), bf16),
-            pltpu.VMEM((pairs, ori_dev), f32),
-            pltpu.VMEM((2 * ori_dev, dom * pairs), bf16),
+        scratch_shapes=[pltpu.VMEM(*column) for column in columns]
+        + [
+            pltpu.VMEM((2 * ori_dev, particles_all * trans), bf16),
+            pltpu.VMEM((particles_all * ori_dev, 2 * pairs), bf16),
             pltpu.VMEM((dom * orients, part_dev, lanes), f32),
-            dma((4,)),
+            dma((3,)),
         ],
         compiler_params=params,
         name="sums",
-    )(images, squares, messages, e)
+    )(far(scaled), far(waves), far(squares), messages, e)
     return (
         posterior.reshape(part_dev, trans, ori_dev),
         image_sums,

time: 38.4 us -> 35.2 us (0.917)
  Pallas kernels: 20.2 us -> 15.7 us
  waiting for transfers between devices: 4.84 us -> 6.84 us
  local copies, waits for them, and re-layouts: 0.7 us -> 0 us
    pallas_call x1, Pallas kernels: 10.2 us -> 8.02 us  [on_device(): pl.pallas_call(functools.partial(score_kernel, chunk, groups), out_shape=...]
    all_to_all x1, waiting for transfers between devices: 4.83 us -> 6.84 us  [on_device(): messages = lax.all_to_all(message, ('dom', 'orient'), 0, 0)]
    pallas_call x2, Pallas kernels: 6.11 us -> 4.13 us  [the longest x1 2.48 us: on_device(): pl.pallas_call(column_kernel, out_shape=tuple((pltpu.HBM(*column) for col...]
    unnamed x4 -> x0, local copies, waits for them, and re-layouts: 0.7 us -> none
  transfers between devices with their start and end apart: 2 -> 2, of which waited for: 1 -> 1; matrix products, arithmetic and copies ran while one was open for 0% -> 0% of each run, Pallas kernels for 39% -> 30%
where the time goes in v3:
time: 35.2 us; the launch traced here: 34.7 us
  Pallas kernels  15.7 us (45%)
  starting transfers between devices  11.5 us (33%)
  waiting for transfers between devices  6.84 us (19%)
  between operations  0.67 us (2%)
    pallas_call x1, Pallas kernels, on_device(): pl.pallas_call(functools.partial(score_kernel, chunk, groups), out_shape=...  8.02 us
    all_to_all x1, waiting for transfers between devices, on_device(): messages = lax.all_to_all(message, ('dom', 'orient'), 0, 0)  6.84 us
    all_to_all x1, starting transfers between devices, on_device(): messages = lax.all_to_all(message, ('dom', 'orient'), 0, 0)  6.33 us
    all_to_all x1, starting transfers between devices, on_device(): recv = lax.all_to_all(send, 'dom', 0, 0)  5.18 us
    pallas_call x1, Pallas kernels, on_device(): pl.pallas_call(functools.partial(sum_kernel, orients, shells, scale), out...  3.56 us
    pallas_call x1, Pallas kernels, on_device(): pl.pallas_call(column_kernel, out_shape=tuple((pltpu.HBM(*column) for col...  2.48 us
    pallas_call x1, Pallas kernels, on_device(): pl.pallas_call(pack_kernel, out_shape=pltpu.VMEM((dom, part_dev, 2, width...  1.64 us
  transfers between devices with their start and end apart: 2, of which 1 were waited for; matrix products, arithmetic and copies ran while one was open for 0% of the time, Pallas kernels for 30%

profile of v3, /device:TPU:0, one launch (start us, length us, event | category | flops | bytes accessed | tf_op | source)
XLA Modules:
  0.0 34.7 jit_solution(1697115781899607950)
XLA Ops:
  0.6 1.6 %pack.1 = bf16[8,8,2,1024]{3,2,1,0:T(2,128)(2,1)} custom-call(bf16[8,2,8192]{2,1,0:T(2,128)(2,1)} %part_hbm.3), custom_call_target="tpu_custom_call" | custom-call | tf_op jit(solution)/shard_map/pack/pallas_call | solution.py:464
  2.3 5.2 %all-to-all-start = ((bf16[8,8,2,1024]{3,2,1,0:T(2,128)(2,1)}), bf16[8,8,2,1024]{3,2,1,0:T(2,128)(2,1)S(1)}, u32[]{:S(2)}, u32[]{:S(2)}) async-start(bf16[8,8,2,1024]{3,2,1,0:T(2,128)(2,1)} %pack.1), calls=%async_computation | async-start | bytes 524288 | tf_op jit(solution)/shard_map/all_to_all | solution.py:473
  7.5 8.0 %scores.1 = (bf16[32,24,128]{2,1,0:T(8,128)(2,1)}, f32[128,16]{1,0:T(8,128)S(1)}) custom-call(s32[64]{0:T(128)} %group_hbm.3, bf16[8,2,8192]{2,1,0:T(2,128)(2,1)} %part_hbm.3, bf16[16,2,8192]{2,1,0:T(2,128)(2,1)} %refs_hbm.1, f32[16,8192]{1,0:T(8,128)} %phase_hbm.3, s32[1,8192]{1,0:T(1,128)} %bitcast.4, s32[8,16]{1,0:T(8,128)} %mask_hbm.1, ...), custom_call_target="tpu_custom_call" | custom-call | tf_op jit(solution)/shard_map/scores/pallas_call | solution.py:476
  15.5 0.0 all-to-all-done.recv_ref
  15.5 6.3 %all-to-all-start.1 = ((bf16[32,24,128]{2,1,0:T(8,128)(2,1)}), bf16[32,24,128]{2,1,0:T(8,128)(2,1)S(1)}, u32[]{:S(2)}, u32[]{:S(2)}) async-start(bf16[32,24,128]{2,1,0:T(8,128)(2,1)} %get-tuple-element.16), calls=%async_computation.1 | async-start | bytes 393216 | tf_op jit(solution)/shard_map/all_to_all | solution.py:516
  21.8 2.5 %columns.1 = (f32[2,64,1024]{2,1,0:T(8,128)}, bf16[32,2048]{1,0:T(8,128)(2,1)}, bf16[1024,128]{1,0:T(8,128)(2,1)}) custom-call(s32[64]{0:T(128)} %group_hbm.3, bf16[8,8,2,1024]{3,2,1,0:T(2,128)(2,1)S(1)} %all-to-all-done.recv_ref, f32[16,8192]{1,0:T(8,128)} %phase_hbm.3, s32[1,8192]{1,0:T(1,128)} %bitcast.5, f32[64,64]{1,0:T(8,128)} %table_hbm.3), custom_call_target="tpu_custom_call" | custom-call | tf_op jit(solution)/shard_map/columns/pallas_call | solution.py:524
  24.3 6.8 %all-to-all-done.1.recv_ref = bf16[32,24,128]{2,1,0:T(8,128)(2,1)S(1)} async-done(((bf16[32,24,128]{2,1,0:T(8,128)(2,1)}), bf16[32,24,128]{2,1,0:T(8,128)(2,1)S(1)}, u32[]{:S(2)}, u32[]{:S(2)}) %all-to-all-start.1) | async-done | bytes 196640 | tf_op jit(solution)/shard_map/all_to_all | solution.py:516
  31.2 3.6 %sums.1 = (f32[128,16]{1,0:T(8,128)}, f32[16,2,1024]{2,1,0:T(2,128)}, f32[16,64]{1,0:T(8,128)}, f32[1,64]{1,0:T(1,128)}) custom-call(f32[2,64,1024]{2,1,0:T(8,128)} %get-tuple-element.13.scaled_hbm, bf16[32,2048]{1,0:T(8,128)(2,1)} %get-tuple-element.14.wave_hbm, bf16[1024,128]{1,0:T(8,128)(2,1)} %get-tuple-element.15.square_hbm, ...), custom_call_target="tpu_custom_call" | custom-call | tf_op jit(solution)/shard_map/sums/pallas_call | solution.py:547
Async XLA Ops:
  2.3 13.2 %all-to-all-start = ((bf16[8,8,2,1024]{3,2,1,0:T(2,128)(2,1)}), bf16[8,8,2,1024]{3,2,1,0:T(2,128)(2,1)S(1)}, u32[]{:S(2)}, u32[]{:S(2)}) async-start(bf16[8,8,2,1024]{3,2,1,0:T(2,128)(2,1)} %pack.1), calls=%async_computation | async-start | bytes 524288 | tf_op jit(solution)/shard_map/all_to_all | solution.py:473
  15.5 15.7 %all-to-all-start.1 = ((bf16[32,24,128]{2,1,0:T(8,128)(2,1)}), bf16[32,24,128]{2,1,0:T(8,128)(2,1)S(1)}, u32[]{:S(2)}, u32[]{:S(2)}) async-start(bf16[32,24,128]{2,1,0:T(8,128)(2,1)} %get-tuple-element.16), calls=%async_computation.1 | async-start | bytes 393216 | tf_op jit(solution)/shard_map/all_to_all | solution.py:516

commit v4 on v3

--- a/solution.py
+++ b/solution.py
@@ -100,7 +100,6 @@
 
 def score_kernel(
     chunk,
-    groups,
     group_hbm,
     part_hbm,
     refs_hbm,
@@ -125,6 +124,8 @@
     planes_ref,
     hot_ref,
     scaled_ref,
+    pix_ref,
+    wave_ref,
     rows_ref,
     small_sems,
     big_sems,
@@ -147,19 +148,7 @@
         ],
         small_sems,
     )
-    big = []
-    for g in range(groups):
-        cols = pl.ds(g * (pixels // groups), pixels // groups)
-        big.append(
-            start_all(
-                [
-                    (part_hbm.at[:, :, cols], part_ref.at[:, :, cols]),
-                    (phase_hbm.at[:, cols], phase_ref.at[:, cols]),
-                    (refs_hbm.at[:, :, cols], refs_ref.at[:, :, cols]),
-                ],
-                big_sems.at[g],
-            )
-        )
+    big = start_all([(phase_hbm, phase_ref), (part_hbm, part_ref), (refs_hbm, refs_ref)], big_sems)
     for copy in small:
         copy.wait()
 
@@ -172,19 +161,25 @@
         [p.astype(f32) for p in pieces(ctf_rows, 3)] + [p.astype(f32) for p in pieces(inverse, 3)], axis=0
     ).astype(bf16)
     n = part_dev
-    norms = None
-    scores = None
     for step in range(blocks):
-        if step % (blocks // groups) == 0:
-            for copy in big[step // (blocks // groups)]:
-                copy.wait()
-        col0 = step * chunk
-        cols = pl.ds(col0, chunk)
+        cols = slice(step * chunk, (step + 1) * chunk)
         hot = one_hot(shell_ref[:, cols], shells)
         hot_ref[:, cols] = hot
         picked = nn(table, hot)
-        ctf_pix = picked[0:n] + picked[n : 2 * n] + picked[2 * n : 3 * n]
-        inv_sigma = picked[3 * n : 3 * n + 8] + picked[3 * n + 8 : 3 * n + 16] + picked[3 * n + 16 : 3 * n + 24]
+        pix_ref[0:n, cols] = picked[0:n] + picked[n : 2 * n] + picked[2 * n : 3 * n]
+        pix_ref[n : n + 8, cols] = picked[3 * n : 3 * n + 8] + picked[3 * n + 8 : 3 * n + 16] + picked[3 * n + 16 : 3 * n + 24]
+    big[0].wait()
+    for t in range(pixels // lanes):
+        cols = slice(t * lanes, (t + 1) * lanes)
+        sine, cosine = sin_cos(phase_ref[:, cols])
+        wave_ref[0:trans, cols] = cosine
+        wave_ref[trans : 2 * trans, cols] = sine
+    big[1].wait()
+    big[2].wait()
+    norms = [None, None]
+    scores = [None, None]
+    for step in range(blocks):
+        col0 = step * chunk
         part0 = step * tiles * part_dev * 2
         refs0 = step * tiles * ori_dev * 2
         split_planes((part_dev, tiles, lambda i, t: part_ref[i, :, pl.ds(col0 + t * lanes, lanes)]), part_rows, part0)
@@ -192,37 +187,43 @@
         squares = []
         weighted = [[], []]
         for t in range(tiles):
-            here = slice(t * lanes, (t + 1) * lanes)
-            tcols = pl.ds(col0 + t * lanes, lanes)
+            cols = slice(col0 + t * lanes, col0 + (t + 1) * lanes)
             part_r = read_plane(part_rows, part0, part_dev, t, 0)
             part_m = read_plane(part_rows, part0, part_dev, t, 1)
             refs_r = read_plane(refs_rows, refs0, ori_dev, t, 0)
             refs_m = read_plane(refs_rows, refs0, ori_dev, t, 1)
-            ctf = ctf_pix[:, here]
-            scaled_ref[0:n, tcols] = part_r * ctf
-            scaled_ref[n : 2 * n, tcols] = part_m * ctf
-            inv = jnp.concatenate([inv_sigma[:, here]] * (ori_dev // 8), axis=0)
+            ctf = pix_ref[0:n, cols]
+            scaled_ref[0:n, cols] = part_r * ctf
+            scaled_ref[n : 2 * n, cols] = part_m * ctf
+            inv = jnp.concatenate([pix_ref[n : n + 8, cols]] * (ori_dev // 8), axis=0)
             for p, plane in enumerate((refs_r, refs_m)):
                 weighted[p].append((plane * inv).astype(bf16))
                 planes_ref[:, pl.ds(2 * col0 + p * chunk + t * lanes, lanes)] = plane.astype(bf16)
             power = jnp.concatenate([refs_r * refs_r + refs_m * refs_m, part_r * part_r + part_m * part_m], axis=0)
             high = power.astype(bf16).astype(f32)
-            squares.append(jnp.concatenate([high, power - high], axis=0).astype(bf16))
-        more = nt(jnp.concatenate(squares, axis=1), hot)
-        norms = more if norms is None else norms + more
+            squares.append((high.astype(bf16), (power - high).astype(bf16)))
         for t in range(tiles):
-            sine, cosine = sin_cos(phase_ref[:, pl.ds(col0 + t * lanes, lanes)])
+            cols = slice(col0 + t * lanes, col0 + (t + 1) * lanes)
 
             def store(p, i, value):
                 at = 2 * col0 + p * chunk + t * lanes
                 img_ref[i * trans : (i + 1) * trans, at : at + lanes] = value
 
-            write_images(store, scaled_ref, col0 + t * lanes, cosine, sine, n)
-        more = nt(img_ref[:, 2 * col0 : 2 * (col0 + chunk)], jnp.concatenate(weighted[0] + weighted[1], axis=1))
-        scores = more if scores is None else scores + more
+            write_images(
+                store, scaled_ref, col0 + t * lanes, wave_ref[0:trans, cols], wave_ref[trans : 2 * trans, cols], n
+            )
+        at = 2 * col0
+        more = nt(img_ref[:, at : at + chunk], jnp.concatenate(weighted[0], axis=1)) + nt(
+            img_ref[:, at + chunk : at + 2 * chunk], jnp.concatenate(weighted[1], axis=1)
+        )
+        scores[0] = more if scores[0] is None else scores[0] + more
+        for p in range(2):
+            more = nt(jnp.concatenate([sq[p] for sq in squares], axis=1), hot_ref[:, col0 : col0 + chunk])
+            norms[p] = more if norms[p] is None else norms[p] + more
+    scores = scores[0]
 
     both = ori_dev + part_dev
-    norms = norms[0:both, :] + norms[both : 2 * both, :]
+    norms = norms[0] + norms[1]
     ref_norm = norms[0:ori_dev]
     part_norm = norms[ori_dev:both]
     ctf_square = ctf_rows * ctf_rows
@@ -251,9 +252,13 @@
             part = mixed[:, p * chunk : (p + 1) * chunk] * img_ref[:, at : at + chunk].astype(f32)
             total = part if total is None else total + part
         folded = total.reshape(part_dev, trans // 8, 8, chunk).sum(axis=1).reshape(part_dev * 8, chunk)
-        more = nt(folded.astype(bf16), hot_ref[:, col0 : col0 + chunk])
-        cross = more if cross is None else cross + more
-    cross = cross.reshape(part_dev, 8, shells).sum(axis=1)
+        folded = folded.astype(bf16)
+        more = [
+            nt(folded[:, k * chunk // 2 : (k + 1) * chunk // 2], hot_ref[:, col0 + k * chunk // 2 : col0 + (k + 1) * chunk // 2])
+            for k in range(2)
+        ]
+        cross = more if cross is None else [old + new for old, new in zip(cross, more)]
+    cross = (cross[0] + cross[1]).reshape(part_dev, 8, shells).sum(axis=1)
     total = jnp.sum(orient_sums, axis=1, keepdims=True)
     third = ctf_square * nn(orient_sums, ref_norm, precision=highest)
     noise = part_norm * total - 2.0 * cross + third
@@ -450,8 +455,7 @@
     orients = lax.axis_size("orient")
     width = pixels // dom
     pairs = part_dev * trans
-    chunk = 2048
-    groups = 1
+    chunk = 4096
     shell_row = shell_index.reshape(1, pixels)
     sigma_row = sigma2.reshape(1, shells)
     vmem = pl.BlockSpec(memory_space=pltpu.VMEM)
@@ -474,9 +478,9 @@
 
     both = ori_dev + part_dev
     message, e = pl.pallas_call(
-        functools.partial(score_kernel, chunk, groups),
+        functools.partial(score_kernel, chunk),
         out_shape=(
-            jax.ShapeDtypeStruct((dom * orients, both, lanes), bf16),
+            pltpu.VMEM((dom * orients, both, lanes), bf16),
             jax.ShapeDtypeStruct((pairs, ori_dev), f32),
         ),
         in_specs=[anywhere] * 8,
@@ -496,9 +500,11 @@
             pltpu.VMEM((ori_dev, 2 * pixels), bf16),
             pltpu.VMEM((shells, pixels), bf16),
             pltpu.VMEM((2 * part_dev, pixels), f32),
+            pltpu.VMEM((part_dev + 8, pixels), f32),
+            pltpu.VMEM((2 * trans, pixels), f32),
             pltpu.VMEM((part_dev, shells), f32),
             dma((5,)),
-            dma((groups, 3)),
+            dma((3,)),
         ],
         compiler_params=params,
         name="scores",

time: 35.2 us -> 34.9 us (level)
  no operation moved by 1% of the time
where the time goes in v4:
time: 34.9 us; the launch traced here: 34.5 us
  Pallas kernels  15.5 us (44%)
  starting transfers between devices  11.5 us (33%)
  waiting for transfers between devices  6.84 us (20%)
  between operations  0.67 us (2%)
    pallas_call x1, Pallas kernels, on_device(): pl.pallas_call(functools.partial(score_kernel, chunk), out_shape=(pltpu.V...  7.78 us
    all_to_all x1, waiting for transfers between devices, on_device(): messages = lax.all_to_all(message, ('dom', 'orient'), 0, 0)  6.84 us
    all_to_all x1, starting transfers between devices, on_device(): messages = lax.all_to_all(message, ('dom', 'orient'), 0, 0)  6.33 us
    all_to_all x1, starting transfers between devices, on_device(): recv = lax.all_to_all(send, 'dom', 0, 0)  5.18 us
    pallas_call x1, Pallas kernels, on_device(): pl.pallas_call(functools.partial(sum_kernel, orients, shells, scale), out...  3.56 us
    pallas_call x1, Pallas kernels, on_device(): pl.pallas_call(column_kernel, out_shape=tuple((pltpu.HBM(*column) for col...  2.48 us
    pallas_call x1, Pallas kernels, on_device(): pl.pallas_call(pack_kernel, out_shape=pltpu.VMEM((dom, part_dev, 2, width...  1.64 us
  transfers between devices with their start and end apart: 2, of which 1 were waited for; matrix products, arithmetic and copies ran while one was open for 0% of the time, Pallas kernels for 30%

profile of v4, /device:TPU:0, one launch (start us, length us, event | category | flops | bytes accessed | tf_op | source)
XLA Modules:
  0.0 34.5 jit_solution(8547355802798521529)
XLA Ops:
  0.6 1.6 %pack.1 = bf16[8,8,2,1024]{3,2,1,0:T(2,128)(2,1)} custom-call(bf16[8,2,8192]{2,1,0:T(2,128)(2,1)} %part_hbm.3), custom_call_target="tpu_custom_call" | custom-call | tf_op jit(solution)/shard_map/pack/pallas_call | solution.py:468
  2.3 5.2 %all-to-all-start = ((bf16[8,8,2,1024]{3,2,1,0:T(2,128)(2,1)}), bf16[8,8,2,1024]{3,2,1,0:T(2,128)(2,1)S(1)}, u32[]{:S(2)}, u32[]{:S(2)}) async-start(bf16[8,8,2,1024]{3,2,1,0:T(2,128)(2,1)} %pack.1), calls=%async_computation | async-start | bytes 524288 | tf_op jit(solution)/shard_map/all_to_all | solution.py:477
  7.5 7.8 %scores.1 = (bf16[32,24,128]{2,1,0:T(8,128)(2,1)}, f32[128,16]{1,0:T(8,128)S(1)}) custom-call(s32[64]{0:T(128)} %group_hbm.3, bf16[8,2,8192]{2,1,0:T(2,128)(2,1)} %part_hbm.3, bf16[16,2,8192]{2,1,0:T(2,128)(2,1)} %refs_hbm.1, f32[16,8192]{1,0:T(8,128)} %phase_hbm.3, s32[1,8192]{1,0:T(1,128)} %bitcast.4, s32[8,16]{1,0:T(8,128)} %mask_hbm.1, ...), custom_call_target="tpu_custom_call" | custom-call | tf_op jit(solution)/shard_map/scores/pallas_call | solution.py:480
  15.3 0.0 all-to-all-done.recv_ref
  15.3 6.3 %all-to-all-start.1 = ((bf16[32,24,128]{2,1,0:T(8,128)(2,1)}), bf16[32,24,128]{2,1,0:T(8,128)(2,1)S(1)}, u32[]{:S(2)}, u32[]{:S(2)}) async-start(bf16[32,24,128]{2,1,0:T(8,128)(2,1)} %get-tuple-element.16), calls=%async_computation.1 | async-start | bytes 393216 | tf_op jit(solution)/shard_map/all_to_all | solution.py:522
  21.6 2.5 %columns.1 = (f32[2,64,1024]{2,1,0:T(8,128)}, bf16[32,2048]{1,0:T(8,128)(2,1)}, bf16[1024,128]{1,0:T(8,128)(2,1)}) custom-call(s32[64]{0:T(128)} %group_hbm.3, bf16[8,8,2,1024]{3,2,1,0:T(2,128)(2,1)S(1)} %all-to-all-done.recv_ref, f32[16,8192]{1,0:T(8,128)} %phase_hbm.3, s32[1,8192]{1,0:T(1,128)} %bitcast.5, f32[64,64]{1,0:T(8,128)} %table_hbm.3), custom_call_target="tpu_custom_call" | custom-call | tf_op jit(solution)/shard_map/columns/pallas_call | solution.py:530
  24.1 6.8 %all-to-all-done.1.recv_ref = bf16[32,24,128]{2,1,0:T(8,128)(2,1)S(1)} async-done(((bf16[32,24,128]{2,1,0:T(8,128)(2,1)}), bf16[32,24,128]{2,1,0:T(8,128)(2,1)S(1)}, u32[]{:S(2)}, u32[]{:S(2)}) %all-to-all-start.1) | async-done | bytes 196640 | tf_op jit(solution)/shard_map/all_to_all | solution.py:522
  30.9 3.6 %sums.1 = (f32[128,16]{1,0:T(8,128)}, f32[16,2,1024]{2,1,0:T(2,128)}, f32[16,64]{1,0:T(8,128)}, f32[1,64]{1,0:T(1,128)}) custom-call(f32[2,64,1024]{2,1,0:T(8,128)} %get-tuple-element.13.scaled_hbm, bf16[32,2048]{1,0:T(8,128)(2,1)} %get-tuple-element.14.wave_hbm, bf16[1024,128]{1,0:T(8,128)(2,1)} %get-tuple-element.15.square_hbm, ...), custom_call_target="tpu_custom_call" | custom-call | tf_op jit(solution)/shard_map/sums/pallas_call | solution.py:553
Async XLA Ops:
  2.3 13.0 %all-to-all-start = ((bf16[8,8,2,1024]{3,2,1,0:T(2,128)(2,1)}), bf16[8,8,2,1024]{3,2,1,0:T(2,128)(2,1)S(1)}, u32[]{:S(2)}, u32[]{:S(2)}) async-start(bf16[8,8,2,1024]{3,2,1,0:T(2,128)(2,1)} %pack.1), calls=%async_computation | async-start | bytes 524288 | tf_op jit(solution)/shard_map/all_to_all | solution.py:477
  15.3 15.7 %all-to-all-start.1 = ((bf16[32,24,128]{2,1,0:T(8,128)(2,1)}), bf16[32,24,128]{2,1,0:T(8,128)(2,1)S(1)}, u32[]{:S(2)}, u32[]{:S(2)}) async-start(bf16[32,24,128]{2,1,0:T(8,128)(2,1)} %get-tuple-element.16), calls=%async_computation.1 | async-start | bytes 393216 | tf_op jit(solution)/shard_map/all_to_all | solution.py:522

commit v5 on v4

--- a/solution.py
+++ b/solution.py
@@ -281,15 +281,13 @@
     phase_hbm,
     shell_hbm,
     table_hbm,
-    scaled_hbm,
-    wave_hbm,
+    scaled_ref,
+    wave_ref,
     square_hbm,
     group_ref,
     phase_ref,
     shell_ref,
     table_ref,
-    scaled_ref,
-    wave_ref,
     square_ref,
     rows_ref,
     planes_ref,
@@ -334,6 +332,8 @@
         .reshape(sources * pairs, 2 * shells)
         .astype(bf16)
     )
+    square_copy = pltpu.make_async_copy(square_ref, square_hbm, sems.at[0])
+    square_copy.start()
     n = part_dev
 
     def source_step(src, carry):
@@ -348,17 +348,15 @@
         return carry
 
     lax.fori_loop(0, sources, source_step, 0, unroll=2)
-    copies = start_all([(scaled_ref, scaled_hbm), (wave_ref, wave_hbm), (square_ref, square_hbm)], sems)
-    for copy in copies:
-        copy.wait()
+    square_copy.wait()
 
 
 def sum_kernel(
     orients,
     shells,
     scale,
-    scaled_hbm,
-    wave_hbm,
+    scaled_ref,
+    wave_ref,
     square_hbm,
     recv_ref,
     e_ref,
@@ -366,19 +364,18 @@
     sums_ref,
     weights_ref,
     noise_ref,
-    scaled_ref,
-    wave_ref,
     square_ref,
     half_ref,
     left_ref,
     share_ref,
-    sems,
+    sem,
 ):
     pairs, ori_dev = e_ref.shape
     part_dev = recv_ref.shape[1] - ori_dev
     trans = pairs // part_dev
     sources = recv_ref.shape[0] // orients
-    copies = start_all([(wave_hbm, wave_ref), (scaled_hbm, scaled_ref), (square_hbm, square_ref)], sems)
+    square_copy = pltpu.make_async_copy(square_hbm, square_ref, sem)
+    square_copy.start()
     me = lax.axis_index("dom")
     mine = lax.axis_index("orient")
     lane_part = lax.broadcasted_iota(jnp.int32, (part_dev, pairs), 1) // trans
@@ -420,8 +417,6 @@
     factor = share_ref[me * orients + mine][:, 0:ori_dev]
     wide = (part_dev, trans, ori_dev)
     post_ref[...] = (e_ref[...].reshape(wide) * jnp.broadcast_to(factor[:, None, :], wide)).reshape(pairs, ori_dev)
-    copies[0].wait()
-    copies[1].wait()
     for tile in range(sums_ref.shape[2] // wave_tile):
         cols = slice(tile * wave_tile, (tile + 1) * wave_tile)
         waves = wave_ref[:, 2 * tile * wave_tile : 2 * (tile + 1) * wave_tile]
@@ -440,7 +435,7 @@
         for p in range(2):
             for j in range(ori_dev):
                 sums_ref[j, p : p + 1, cols] = sums[p][j : j + 1, :]
-    copies[2].wait()
+    square_copy.wait()
     weights = nn(half_ref[...], square_ref[...])
     weights = weights[0:ori_dev] + weights[ori_dev : 2 * ori_dev]
     weights_ref[...] = weights[:, 0:shells] + weights[:, shells : 2 * shells]
@@ -529,17 +524,17 @@
     )
     scaled, waves, squares = pl.pallas_call(
         column_kernel,
-        out_shape=tuple(pltpu.HBM(*column) for column in columns),
+        out_shape=(pltpu.VMEM(*columns[0]), pltpu.VMEM(*columns[1]), pltpu.HBM(*columns[2])),
         in_specs=[anywhere, vmem] + [anywhere] * 3,
-        out_specs=(anywhere,) * 3,
+        out_specs=(vmem, vmem, anywhere),
         scratch_shapes=[
             pltpu.SMEM(ctf_group.shape, jnp.int32),
             pltpu.VMEM((trans, width), f32),
             pltpu.VMEM((1, width), jnp.int32),
             pltpu.VMEM(ctf_table.shape, f32),
         ]
-        + [pltpu.VMEM(*column) for column in columns]
         + [
+            pltpu.VMEM(*columns[2]),
             pltpu.VMEM((particles_all, shells), f32),
             pltpu.VMEM((particles_all * 2 * width // lanes, lanes), f32),
             pltpu.VMEM((particles_all, width), f32),
@@ -558,18 +553,18 @@
             jax.ShapeDtypeStruct((ori_dev, shells), f32),
             jax.ShapeDtypeStruct((1, shells), f32),
         ),
-        in_specs=[anywhere, anywhere, anywhere, vmem, vmem],
+        in_specs=[vmem, vmem, anywhere, vmem, vmem],
         out_specs=(vmem, vmem, vmem, vmem),
-        scratch_shapes=[pltpu.VMEM(*column) for column in columns]
-        + [
+        scratch_shapes=[
+            pltpu.VMEM(*columns[2]),
             pltpu.VMEM((2 * ori_dev, particles_all * trans), bf16),
             pltpu.VMEM((particles_all * ori_dev, 2 * pairs), bf16),
             pltpu.VMEM((dom * orients, part_dev, lanes), f32),
-            dma((3,)),
+            dma,
         ],
         compiler_params=params,
         name="sums",
-    )(far(scaled), far(waves), far(squares), messages, e)
+    )(scaled, waves, far(squares), messages, e)
     return (
         posterior.reshape(part_dev, trans, ori_dev),
         image_sums,

time: 34.9 us -> 33.7 us (0.966)
  Pallas kernels: 15.5 us -> 13.7 us
  waiting for transfers between devices: 6.84 us -> 7.43 us
    pallas_call x1, Pallas kernels: 3.56 us -> 2.43 us  [on_device(): pl.pallas_call(functools.partial(sum_kernel, orients, shells, scale), out...]
    all_to_all x1, waiting for transfers between devices: 6.84 us -> 7.43 us  [on_device(): messages = lax.all_to_all(message, ('dom', 'orient'), 0, 0)]
    pallas_call x1, Pallas kernels: 2.48 us -> 1.89 us  [on_device(): pl.pallas_call(column_kernel, out_shape=(pltpu.VMEM(*columns[0]), pltpu.V...]
  transfers between devices with their start and end apart: 2 -> 2, of which waited for: 1 -> 1; matrix products, arithmetic and copies ran while one was open for 0% -> 0% of each run, Pallas kernels for 30% -> 29%
where the time goes in v5:
time: 33.7 us; the launch traced here: 33.3 us
  Pallas kernels  13.7 us (41%)
  starting transfers between devices  11.5 us (34%)
  waiting for transfers between devices  7.43 us (22%)
  between operations  0.67 us (2%)
    pallas_call x1, Pallas kernels, on_device(): pl.pallas_call(functools.partial(score_kernel, chunk), out_shape=(pltpu.V...  7.74 us
    all_to_all x1, waiting for transfers between devices, on_device(): messages = lax.all_to_all(message, ('dom', 'orient'), 0, 0)  7.43 us
    all_to_all x1, starting transfers between devices, on_device(): messages = lax.all_to_all(message, ('dom', 'orient'), 0, 0)  6.33 us
    all_to_all x1, starting transfers between devices, on_device(): recv = lax.all_to_all(send, 'dom', 0, 0)  5.18 us
    pallas_call x1, Pallas kernels, on_device(): pl.pallas_call(functools.partial(sum_kernel, orients, shells, scale), out...  2.43 us
    pallas_call x1, Pallas kernels, on_device(): pl.pallas_call(column_kernel, out_shape=(pltpu.VMEM(*columns[0]), pltpu.V...  1.89 us
    pallas_call x1, Pallas kernels, on_device(): pl.pallas_call(pack_kernel, out_shape=pltpu.VMEM((dom, part_dev, 2, width...  1.64 us
  transfers between devices with their start and end apart: 2, of which 1 were waited for; matrix products, arithmetic and copies ran while one was open for 0% of the time, Pallas kernels for 29%

profile of v5, /device:TPU:0, one launch (start us, length us, event | category | flops | bytes accessed | tf_op | source)
XLA Modules:
  0.0 33.3 jit_solution(1881473633556128961)
XLA Ops:
  0.6 1.6 %pack.1 = bf16[8,8,2,1024]{3,2,1,0:T(2,128)(2,1)} custom-call(bf16[8,2,8192]{2,1,0:T(2,128)(2,1)} %part_hbm.3), custom_call_target="tpu_custom_call" | custom-call | tf_op jit(solution)/shard_map/pack/pallas_call | solution.py:463
  2.3 5.2 %all-to-all-start = ((bf16[8,8,2,1024]{3,2,1,0:T(2,128)(2,1)}), bf16[8,8,2,1024]{3,2,1,0:T(2,128)(2,1)S(1)}, u32[]{:S(2)}, u32[]{:S(2)}) async-start(bf16[8,8,2,1024]{3,2,1,0:T(2,128)(2,1)} %pack.1), calls=%async_computation | async-start | bytes 524288 | tf_op jit(solution)/shard_map/all_to_all | solution.py:472
  7.5 7.7 %scores.1 = (bf16[32,24,128]{2,1,0:T(8,128)(2,1)}, f32[128,16]{1,0:T(8,128)S(1)}) custom-call(s32[64]{0:T(128)} %group_hbm.3, bf16[8,2,8192]{2,1,0:T(2,128)(2,1)} %part_hbm.3, bf16[16,2,8192]{2,1,0:T(2,128)(2,1)} %refs_hbm.1, f32[16,8192]{1,0:T(8,128)} %phase_hbm.3, s32[1,8192]{1,0:T(1,128)} %bitcast.4, s32[8,16]{1,0:T(8,128)} %mask_hbm.1, ...), custom_call_target="tpu_custom_call" | custom-call | tf_op jit(solution)/shard_map/scores/pallas_call | solution.py:475
  15.2 0.0 all-to-all-done.recv_ref
  15.2 6.3 %all-to-all-start.1 = ((bf16[32,24,128]{2,1,0:T(8,128)(2,1)}), bf16[32,24,128]{2,1,0:T(8,128)(2,1)S(1)}, u32[]{:S(2)}, u32[]{:S(2)}) async-start(bf16[32,24,128]{2,1,0:T(8,128)(2,1)} %get-tuple-element.16), calls=%async_computation.1 | async-start | bytes 393216 | tf_op jit(solution)/shard_map/all_to_all | solution.py:517
  21.6 1.9 %columns.1 = (f32[2,64,1024]{2,1,0:T(8,128)S(1)}, bf16[32,2048]{1,0:T(8,128)(2,1)S(1)}, bf16[1024,128]{1,0:T(8,128)(2,1)}) custom-call(s32[64]{0:T(128)} %group_hbm.3, bf16[8,8,2,1024]{3,2,1,0:T(2,128)(2,1)S(1)} %all-to-all-done.recv_ref, f32[16,8192]{1,0:T(8,128)} %phase_hbm.3, s32[1,8192]{1,0:T(1,128)} %bitcast.5, f32[64,64]{1,0:T(8,128)} %table_hbm.3), custom_call_target="tpu_custom_call" | custom-call | tf_op jit(solution)/shard_map/columns/pallas_call | solution.py:525
  23.5 7.4 %all-to-all-done.1.recv_ref = bf16[32,24,128]{2,1,0:T(8,128)(2,1)S(1)} async-done(((bf16[32,24,128]{2,1,0:T(8,128)(2,1)}), bf16[32,24,128]{2,1,0:T(8,128)(2,1)S(1)}, u32[]{:S(2)}, u32[]{:S(2)}) %all-to-all-start.1) | async-done | bytes 196640 | tf_op jit(solution)/shard_map/all_to_all | solution.py:517
  30.9 2.4 %sums.1 = (f32[128,16]{1,0:T(8,128)}, f32[16,2,1024]{2,1,0:T(2,128)}, f32[16,64]{1,0:T(8,128)}, f32[1,64]{1,0:T(1,128)}) custom-call(f32[2,64,1024]{2,1,0:T(8,128)S(1)} %get-tuple-element.13.scaled_ref, bf16[32,2048]{1,0:T(8,128)(2,1)S(1)} %get-tuple-element.14.wave_ref, bf16[1024,128]{1,0:T(8,128)(2,1)} %get-tuple-element.15.square_hbm, ...), custom_call_target="tpu_custom_call" | custom-call | tf_op jit(solution)/shard_map/sums/pallas_call | solution.py:548
Async XLA Ops:
  2.3 12.9 %all-to-all-start = ((bf16[8,8,2,1024]{3,2,1,0:T(2,128)(2,1)}), bf16[8,8,2,1024]{3,2,1,0:T(2,128)(2,1)S(1)}, u32[]{:S(2)}, u32[]{:S(2)}) async-start(bf16[8,8,2,1024]{3,2,1,0:T(2,128)(2,1)} %pack.1), calls=%async_computation | async-start | bytes 524288 | tf_op jit(solution)/shard_map/all_to_all | solution.py:472
  15.2 15.7 %all-to-all-start.1 = ((bf16[32,24,128]{2,1,0:T(8,128)(2,1)}), bf16[32,24,128]{2,1,0:T(8,128)(2,1)S(1)}, u32[]{:S(2)}, u32[]{:S(2)}) async-start(bf16[32,24,128]{2,1,0:T(8,128)(2,1)} %get-tuple-element.16), calls=%async_computation.1 | async-start | bytes 393216 | tf_op jit(solution)/shard_map/all_to_all | solution.py:517

commit v6 on v5

--- a/solution.py
+++ b/solution.py
@@ -489,8 +489,8 @@
             pltpu.VMEM(ctf_table.shape, f32),
             pltpu.VMEM((1, shells), f32),
             pltpu.SMEM(ctf_group.shape, jnp.int32),
-            pltpu.VMEM((pixels // lanes * part_dev * 2, lanes), f32),
-            pltpu.VMEM((pixels // lanes * ori_dev * 2, lanes), f32),
+            pltpu.VMEM((pixels // lanes * part_dev * 2 + 8, lanes), f32),
+            pltpu.VMEM((pixels // lanes * ori_dev * 2 + 8, lanes), f32),
             pltpu.VMEM((pairs, 2 * pixels), bf16),
             pltpu.VMEM((ori_dev, 2 * pixels), bf16),
             pltpu.VMEM((shells, pixels), bf16),
@@ -536,7 +536,7 @@
         + [
             pltpu.VMEM(*columns[2]),
             pltpu.VMEM((particles_all, shells), f32),
-            pltpu.VMEM((particles_all * 2 * width // lanes, lanes), f32),
+            pltpu.VMEM((particles_all * 2 * width // lanes + 8, lanes), f32),
             pltpu.VMEM((particles_all, width), f32),
             dma((4,)),
         ],

time: 33.7 us -> 33.7 us (level)
  no operation moved by 1% of the time
where the time goes in v6:
time: 33.7 us; the launch traced here: 33.3 us
  Pallas kernels  13.7 us (41%)
  starting transfers between devices  11.5 us (34%)
  waiting for transfers between devices  7.43 us (22%)
  between operations  0.67 us (2%)
    pallas_call x1, Pallas kernels, on_device(): pl.pallas_call(functools.partial(score_kernel, chunk), out_shape=(pltpu.V...  7.75 us
    all_to_all x1, waiting for transfers between devices, on_device(): messages = lax.all_to_all(message, ('dom', 'orient'), 0, 0)  7.43 us
    all_to_all x1, starting transfers between devices, on_device(): messages = lax.all_to_all(message, ('dom', 'orient'), 0, 0)  6.33 us
    all_to_all x1, starting transfers between devices, on_device(): recv = lax.all_to_all(send, 'dom', 0, 0)  5.18 us
    pallas_call x1, Pallas kernels, on_device(): pl.pallas_call(functools.partial(sum_kernel, orients, shells, scale), out...  2.42 us
    pallas_call x1, Pallas kernels, on_device(): pl.pallas_call(column_kernel, out_shape=(pltpu.VMEM(*columns[0]), pltpu.V...  1.9 us
    pallas_call x1, Pallas kernels, on_device(): pl.pallas_call(pack_kernel, out_shape=pltpu.VMEM((dom, part_dev, 2, width...  1.64 us
  transfers between devices with their start and end apart: 2, of which 1 were waited for; matrix products, arithmetic and copies ran while one was open for 0% of the time, Pallas kernels for 29%

profile of v6, /device:TPU:0, one launch (start us, length us, event | category | flops | bytes accessed | tf_op | source)
XLA Modules:
  0.0 33.3 jit_solution(3485486540470532869)
XLA Ops:
  0.6 1.6 %pack.1 = bf16[8,8,2,1024]{3,2,1,0:T(2,128)(2,1)} custom-call(bf16[8,2,8192]{2,1,0:T(2,128)(2,1)} %part_hbm.3), custom_call_target="tpu_custom_call" | custom-call | tf_op jit(solution)/shard_map/pack/pallas_call | solution.py:463
  2.3 5.2 %all-to-all-start = ((bf16[8,8,2,1024]{3,2,1,0:T(2,128)(2,1)}), bf16[8,8,2,1024]{3,2,1,0:T(2,128)(2,1)S(1)}, u32[]{:S(2)}, u32[]{:S(2)}) async-start(bf16[8,8,2,1024]{3,2,1,0:T(2,128)(2,1)} %pack.1), calls=%async_computation | async-start | bytes 524288 | tf_op jit(solution)/shard_map/all_to_all | solution.py:472
  7.5 7.8 %scores.1 = (bf16[32,24,128]{2,1,0:T(8,128)(2,1)}, f32[128,16]{1,0:T(8,128)S(1)}) custom-call(s32[64]{0:T(128)} %group_hbm.3, bf16[8,2,8192]{2,1,0:T(2,128)(2,1)} %part_hbm.3, bf16[16,2,8192]{2,1,0:T(2,128)(2,1)} %refs_hbm.1, f32[16,8192]{1,0:T(8,128)} %phase_hbm.3, s32[1,8192]{1,0:T(1,128)} %bitcast.4, s32[8,16]{1,0:T(8,128)} %mask_hbm.1, ...), custom_call_target="tpu_custom_call" | custom-call | tf_op jit(solution)/shard_map/scores/pallas_call | solution.py:475
  15.2 0.0 all-to-all-done.recv_ref
  15.2 6.3 %all-to-all-start.1 = ((bf16[32,24,128]{2,1,0:T(8,128)(2,1)}), bf16[32,24,128]{2,1,0:T(8,128)(2,1)S(1)}, u32[]{:S(2)}, u32[]{:S(2)}) async-start(bf16[32,24,128]{2,1,0:T(8,128)(2,1)} %get-tuple-element.16), calls=%async_computation.1 | async-start | bytes 393216 | tf_op jit(solution)/shard_map/all_to_all | solution.py:517
  21.6 1.9 %columns.1 = (f32[2,64,1024]{2,1,0:T(8,128)S(1)}, bf16[32,2048]{1,0:T(8,128)(2,1)S(1)}, bf16[1024,128]{1,0:T(8,128)(2,1)}) custom-call(s32[64]{0:T(128)} %group_hbm.3, bf16[8,8,2,1024]{3,2,1,0:T(2,128)(2,1)S(1)} %all-to-all-done.recv_ref, f32[16,8192]{1,0:T(8,128)} %phase_hbm.3, s32[1,8192]{1,0:T(1,128)} %bitcast.5, f32[64,64]{1,0:T(8,128)} %table_hbm.3), custom_call_target="tpu_custom_call" | custom-call | tf_op jit(solution)/shard_map/columns/pallas_call | solution.py:525
  23.5 7.4 %all-to-all-done.1.recv_ref = bf16[32,24,128]{2,1,0:T(8,128)(2,1)S(1)} async-done(((bf16[32,24,128]{2,1,0:T(8,128)(2,1)}), bf16[32,24,128]{2,1,0:T(8,128)(2,1)S(1)}, u32[]{:S(2)}, u32[]{:S(2)}) %all-to-all-start.1) | async-done | bytes 196640 | tf_op jit(solution)/shard_map/all_to_all | solution.py:517
  30.9 2.4 %sums.1 = (f32[128,16]{1,0:T(8,128)}, f32[16,2,1024]{2,1,0:T(2,128)}, f32[16,64]{1,0:T(8,128)}, f32[1,64]{1,0:T(1,128)}) custom-call(f32[2,64,1024]{2,1,0:T(8,128)S(1)} %get-tuple-element.13.scaled_ref, bf16[32,2048]{1,0:T(8,128)(2,1)S(1)} %get-tuple-element.14.wave_ref, bf16[1024,128]{1,0:T(8,128)(2,1)} %get-tuple-element.15.square_hbm, ...), custom_call_target="tpu_custom_call" | custom-call | tf_op jit(solution)/shard_map/sums/pallas_call | solution.py:548
Async XLA Ops:
  2.3 12.9 %all-to-all-start = ((bf16[8,8,2,1024]{3,2,1,0:T(2,128)(2,1)}), bf16[8,8,2,1024]{3,2,1,0:T(2,128)(2,1)S(1)}, u32[]{:S(2)}, u32[]{:S(2)}) async-start(bf16[8,8,2,1024]{3,2,1,0:T(2,128)(2,1)} %pack.1), calls=%async_computation | async-start | bytes 524288 | tf_op jit(solution)/shard_map/all_to_all | solution.py:472
  15.2 15.7 %all-to-all-start.1 = ((bf16[32,24,128]{2,1,0:T(8,128)(2,1)}), bf16[32,24,128]{2,1,0:T(8,128)(2,1)S(1)}, u32[]{:S(2)}, u32[]{:S(2)}) async-start(bf16[32,24,128]{2,1,0:T(8,128)(2,1)} %get-tuple-element.16), calls=%async_computation.1 | async-start | bytes 393216 | tf_op jit(solution)/shard_map/all_to_all | solution.py:517
